TPU v7x, 512 devices: a whole 4x8x8 slice. The times are simulated.
512 devices in a mesh: batch: 4 (over z_hi, core), patch: 128 (over y, x, z_lo).
Axes of the slice: x: 4, y: 8, z: 8 (z_hi: 2, z_lo: 4; z = z_hi * 4 + z_lo), core: 2. Of those that a mesh axis runs over, the one named last changes fastest.
Arguments:
- latent: bfloat16 [512, 32, 640], P(('batch', 'patch')), parts along dimension 0, may hold values from -45 to 45
- stale_hidden: bfloat16 [16384, 640], P(('batch', 'patch')), parts along dimension 0, may hold values from -5 to 5
- input_proj: bfloat16 [640, 640], replicated, may hold values from -0.25 to 0.25
- query_proj: bfloat16 [640, 640], replicated, may hold values from -20 to 20
- key_proj: bfloat16 [640, 640], replicated, may hold values from -1 to 1
- value_proj: bfloat16 [640, 640], replicated, may hold values from -0.25 to 0.25
- output_proj: bfloat16 [640, 640], replicated, may hold values from -0.25 to 0.25
Outputs:
- level_out: bfloat16 [512, 32, 640], P(('batch', 'patch')), parts along dimension 0
- next_hidden: bfloat16 [16384, 640], P(('batch', 'patch')), parts along dimension 0
There are 4 independent parts, one for each index of `batch`. A program takes and returns all parts, laid end to end along the dimension named above; an argument that names none is the same for every part. Nothing has to cross between parts.
All inputs are finite; a program needn't handle non-finite values.
Results may differ from a plain program's by a relative error of at most 0.0051.
Values may be sent and summed in bfloat16 or wider, within the bound.
No kernel may reach another device: no remote copies, remote signals or barrier semaphores. Data moves between devices by JAX's collectives and lax.ppermute only.
A program may use at most 128 MiB of HBM per device.

v0:
```python
import math

import jax
import jax.numpy as jnp
from jax import lax
from jax.sharding import PartitionSpec as P

HEADS = 10
GROUPS = 32


def layer_norm(projected):
    center = jnp.mean(projected, axis=-1, keepdims=True)
    spread = jnp.mean(jnp.square(projected - center), axis=-1, keepdims=True)
    return ((projected - center) * lax.rsqrt(spread + 1e-05)).astype(jnp.bfloat16)


def on_device(latent, stale_hidden, input_proj, query_proj, key_proj, value_proj, output_proj):
    rows_here, cols_here, channels = latent.shape
    patches = lax.axis_size("patch")
    tok_here = rows_here * cols_here
    groups = GROUPS
    group_width = channels // groups
    cell_values = latent.astype(jnp.float32).reshape(tok_here, groups, group_width)
    cell_count = tok_here * patches * group_width
    center = lax.psum(jnp.sum(cell_values, axis=(0, 2)), "patch") / cell_count
    deviation = cell_values - center[None, :, None]
    spread = lax.psum(jnp.sum(jnp.square(deviation), axis=(0, 2)), "patch") / cell_count
    normed = (deviation * lax.rsqrt(spread + 1e-06)[None, :, None]).reshape(tok_here, channels)
    normed = normed.astype(jnp.bfloat16)
    projected = jnp.dot(normed, input_proj, preferred_element_type=jnp.float32)
    next_hidden = layer_norm(projected)
    pair_proj = jnp.concatenate((key_proj, value_proj), axis=1)
    queries = jnp.dot(next_hidden, query_proj, preferred_element_type=jnp.float32).astype(
        jnp.bfloat16
    )
    fresh_pair = jnp.dot(next_hidden, pair_proj, preferred_element_type=jnp.float32).astype(
        jnp.bfloat16
    )
    stale_pair = jnp.dot(
        lax.all_gather(stale_hidden, "patch", axis=0, tiled=True),
        pair_proj,
        preferred_element_type=jnp.float32,
    ).astype(jnp.bfloat16)
    band_offset = lax.axis_index("patch") * tok_here
    key_values = lax.dynamic_update_slice_in_dim(stale_pair, fresh_pair, band_offset, 0)
    all_tokens = key_values.shape[0]
    head_count = HEADS
    head_width = channels // head_count
    key_rows = key_values[:, :channels].reshape(all_tokens, head_count, head_width)
    value_rows = key_values[:, channels:].reshape(all_tokens, head_count, head_width)
    query_rows = queries.reshape(tok_here, head_count, head_width)
    scores = jnp.einsum("qhd,khd->hqk", query_rows, key_rows, preferred_element_type=jnp.float32)
    scores = scores * (1.0 / math.sqrt(head_width))
    row_max = jnp.max(scores, axis=-1, keepdims=True)
    weights = jnp.exp(scores - row_max)
    row_total = jnp.sum(weights, axis=-1, keepdims=True)
    probs = (weights / row_total).astype(jnp.bfloat16)
    attended = jnp.einsum("hqk,khd->qhd", probs, value_rows, preferred_element_type=jnp.float32)
    attended = attended.reshape(tok_here, channels).astype(jnp.bfloat16)
    mixed_out = jnp.dot(attended, output_proj, preferred_element_type=jnp.float32)
    level_sum = latent.astype(jnp.float32).reshape(tok_here, channels) + projected + mixed_out
    level_out = level_sum.reshape(rows_here, cols_here, channels).astype(jnp.bfloat16)
    return (level_out, next_hidden)


def solution(mesh):
    return jax.shard_map(
        on_device,
        mesh=mesh,
        in_specs=(
            P(("batch", "patch"), None, None),
            P(("batch", "patch"), None),
            P(),
            P(),
            P(),
            P(),
            P(),
        ),
        out_specs=(P(("batch", "patch"), None, None), P(("batch", "patch"), None)),
        check_vma=False,
    )
```

profile of v0, /device:TPU:64, one launch (start us, length us, event | category | flops | bytes accessed | tf_op | source)
XLA Modules:
  0.0 800.6 jit_solution(12911055714066165622)
XLA Ops:
  7.2 0.7 all-gather.2.cloned.1.call-update
  7.9 0.8 convert_reduce_fusion
  8.8 0.1 reduce_sum.61
  8.9 366.8 %psum.14 = f32[32]{0:T(128)S(1)} all-reduce(f32[32]{0:T(128)S(1)} %reduce_sum.61), channel_id=1, replica_groups=mesh['batch'=4,'patch'=128] {'patch'}, use_global_device_ids=true, to_apply=%region_2.0 | all-reduce | flops 32 | bytes 256 | tf_op jit(solution)/shard_map/psum | solution.py:26
  375.9 0.8 fusion.14
  376.8 0.1 reduce_sum.64
  376.9 367.2 %psum.15 = f32[32]{0:T(128)S(1)} all-reduce(f32[32]{0:T(128)S(1)} %reduce_sum.64), channel_id=1, replica_groups=mesh['batch'=4,'patch'=128] {'patch'}, use_global_device_ids=true, to_apply=%region_5.0 | all-reduce | flops 32 | bytes 256 | tf_op jit(solution)/shard_map/psum | solution.py:28
  744.3 1.1 fusion.22
  745.5 0.2 multiply_reduce_fusion
  745.7 1.2 constant_dynamic-update-slice_fusion.1
  746.9 1.3 constant_dynamic-update-slice_fusion
  748.3 0.3 convolution_convert_fusion.1
  748.6 0.2 copy.14
  748.9 1.4 convolution_convert_fusion.2
  750.3 0.1 reshape.46
  750.5 13.4 %fusion.1 = bf16[4096,1280]{0,1:T(8,128)(2,1)} fusion(bf16[640,1280]{1,0:T(8,128)(2,1)S(1)} %constant_dynamic-update-slice_fusion, bf16[4096,640]{1,0:T(8,128)(2,1)} %all-gather.2.cloned.1.call-done), kind=kOutput, calls=%fused_computation.2 | convolution fusion | flops 6716129280 | bytes 17367040 | tf_op jit(solution)/shard_map/dot_general | solution.py:40
  763.9 5.1 dynamic_update_slice.3
  769.0 9.6 %fusion.21 = (bf16[4096,640]{0,1:T(8,128)(2,1)}, bf16[4096,640]{0,1:T(8,128)(2,1)}) fusion(bf16[4096,1280]{0,1:T(8,128)(2,1)} %dynamic_update_slice.3), kind=kLoop, calls=%fused_computation.37 | loop fusion | bytes 20971520 | tf_op jit(solution)/shard_map/slice | solution.py:50
  778.6 3.4 convolution_multiply_fusion
  782.0 2.3 copy-done.1
  784.3 1.0 fusion.23
  785.3 7.3 fusion.6
  792.7 0.1 convert_element_type.50
  792.8 0.9 fusion.8
  (23 shorter events, 0.8 us)
Async XLA Ops:
  7.2 737.2 %copy-start = (bf16[640,640]{1,0:T(8,128)(2,1)S(1)}, bf16[640,640]{1,0:T(8,128)(2,1)}, u32[]{:S(2)}) copy-start(bf16[640,640]{1,0:T(8,128)(2,1)} %param.9) | copy-start | bytes 2457604
  7.2 743.3 %all-gather.2.cloned.1.call-start = ((), (), s32[]{:S(2)}) async-start(), calls=%async_computation | async-start | bytes 5283840 | tf_op jit(solution)/shard_map/all_gather | solution.py:41
  748.3 15.6 %copy-start.4 = (bf16[32,640]{1,0:T(8,128)(2,1)}, bf16[32,640]{1,0:T(8,128)(2,1)S(1)}, u32[]{:S(2)}) copy-start(bf16[32,640]{1,0:T(8,128)(2,1)S(1)} %multiply_convert_fusion) | copy-start | bytes 122884
  782.0 2.3 copy-start.1
  785.3 7.5 copy-start.2
  785.3 7.5 copy-start.3
Sparse Core Ops, SparseCore 0:
  10.1 698.1 all-gather.1
where the time goes:
time: 801 us
  blocking collectives  734 us (92%)
  matrix products  27.9 us (3%)
  local copies, waits for them, and re-layouts  20.6 us (3%)
  between operations  14.2 us (2%)
    psum x1, blocking collectives, on_device(): lax.psum(jnp.sum(jnp.square(deviation), axis=(0, 2)), 'patch') / cell_count  367 us
    psum x1, blocking collectives, on_device(): center = lax.psum(jnp.sum(cell_values, axis=(0, 2)), 'patch') / cell_count  367 us
  transfers between devices with their start and end apart: 1, of which 0 were waited for; matrix products, arithmetic and copies ran while one was open for 1% of the time, Pallas kernels for 0%

commit v1 on v0

v1 whole, which is shorter than its diff:
```python
import math

import jax
import jax.numpy as jnp
from jax import lax
from jax.experimental import pallas as pl
from jax.experimental.pallas import tpu as pltpu
from jax.sharding import PartitionSpec as P

C = 640
HEADS = 10
HEAD = 64
GROUP = 20
TOK = 32
BANDS = 128
LANES = 128
SLOT = 32
WIDE = C + LANES
STEP = math.log2(math.e) / math.sqrt(HEAD)
FAR = -1e30

PLACES = [(y, x, z) for y in range(8) for x in range(4) for z in range(4)]


def _groups(key):
    members = {}
    for index, place in enumerate(PLACES):
        members.setdefault(key(*place), []).append(index)
    return [members[k] for k in sorted(members)]


CUBES = _groups(lambda y, x, z: (y // 2, x // 2, z // 2))
CORNERS = _groups(lambda y, x, z: (y % 2, x % 2, z % 2))
NQ = len(CUBES[0])
NK = len(CORNERS[0])
QROWS = NQ * TOK
KROWS = NK * TOK
BF = jnp.bfloat16
F32 = jnp.float32


def _iota(shape, axis):
    return lax.broadcasted_iota(jnp.int32, shape, axis)


def _pieces(value):
    first = value.astype(BF).astype(F32)
    rest = value - first
    second = rest.astype(BF).astype(F32)
    return first, second, rest - second


def stats_kernel(latent_ref, out_ref):
    cells = latent_ref[...].astype(F32).reshape(QROWS, C)
    center = jnp.sum(cells, axis=0, keepdims=True) * (1.0 / QROWS)
    away = jnp.sum(jnp.square(cells - center), axis=0, keepdims=True)
    out_ref[0:1, :] = center
    out_ref[1:2, :] = away


def _group_mean(row, same_group):
    first, second, third = _pieces(row)
    which = _iota((16, C), 0)
    stacked = jnp.where(which == 0, first, jnp.where(which == 1, second, jnp.where(which == 2, third, 0.0)))
    sums = jnp.dot(stacked.astype(BF), same_group, preferred_element_type=F32)
    return jnp.sum(sums, axis=0, keepdims=True) * (1.0 / GROUP)


def _attend(q_pair, k_pair, v_pair, bias):
    rows = q_pair.shape[0]
    left = _iota((rows, LANES), 1) < HEAD
    zero = jnp.zeros_like(q_pair)
    both = jnp.concatenate([jnp.where(left, q_pair, zero), jnp.where(left, zero, q_pair)], axis=0)
    scores = lax.dot_general(both, k_pair, (((1,), (1,)), ((), ())), preferred_element_type=F32)
    if bias is not None:
        scores = scores + bias
    top = jnp.max(scores, axis=1, keepdims=True)
    weights = jnp.exp2((scores - top) * STEP).astype(BF)
    ones = jnp.ones_like(v_pair)
    sums = jnp.dot(weights, jnp.concatenate([v_pair, ones], axis=1), preferred_element_type=F32)
    total = sums[:, LANES:]
    mixed = sums[:, :LANES] / total
    logs = top * STEP + jnp.log2(total)
    return jnp.where(left, mixed[:rows], mixed[rows:]), logs[:rows], logs[rows:]


def _pack_logs(logs):
    first, second, third = _pieces(logs)
    lane = _iota(logs.shape, 1)
    return jnp.where(lane < SLOT, first, jnp.where(lane < 2 * SLOT, second, third)).astype(BF)


def main_kernel(
    place_ref,
    latent_ref,
    stats_ref,
    stale_ref,
    input_ref,
    query_ref,
    key_ref,
    value_ref,
    part_ref,
    own_ref,
    projected_ref,
    hidden_ref,
    projected_all,
    hidden_all,
    queries,
):
    mine = pl.multiple_of(place_ref[0] * TOK, TOK)
    band = place_ref[1]

    stats = stats_ref[...]
    parts_mean = stats[:, 0, :]
    parts_away = stats[:, 1, :]
    mean = jnp.sum(parts_mean, axis=0, keepdims=True) * (1.0 / NK)
    away = jnp.sum(parts_away + float(QROWS) * jnp.square(parts_mean - mean), axis=0, keepdims=True)
    row_group = (_iota((C, C), 0) * 52429) >> 20
    col_group = (_iota((C, C), 1) * 52429) >> 20
    same_group = jnp.where(row_group == col_group, 1.0, 0.0).astype(BF)
    center = _group_mean(mean, same_group)
    spread = _group_mean(away * (1.0 / (QROWS * NK)) + jnp.square(mean - center), same_group)
    gain = lax.rsqrt(spread + 1e-06)
    cells = latent_ref[...].astype(F32).reshape(QROWS, C)
    normed = ((cells - center) * gain).astype(BF)

    projected = jnp.dot(normed, input_ref[...], preferred_element_type=F32)
    projected_all[...] = projected
    row_mean = jnp.mean(projected, axis=1, keepdims=True)
    shifted = projected - row_mean
    row_spread = jnp.mean(jnp.square(shifted), axis=1, keepdims=True)
    hidden = (shifted * lax.rsqrt(row_spread + 1e-05)).astype(BF)
    hidden_all[...] = hidden
    projected_ref[...] = projected_all[pl.ds(mine, TOK), :]
    own_hidden = hidden_all[pl.ds(mine, TOK), :]
    hidden_ref[...] = own_hidden
    queries[...] = jnp.dot(hidden, query_ref[...], preferred_element_type=F32).astype(BF)

    stale = stale_ref[...].reshape(KROWS, C)
    keys = jnp.dot(stale, key_ref[...], preferred_element_type=F32).astype(BF)
    values = jnp.dot(stale, value_ref[...], preferred_element_type=F32).astype(BF)
    fresh_keys = jnp.dot(own_hidden, key_ref[...], preferred_element_type=F32).astype(BF)
    fresh_values = jnp.dot(own_hidden, value_ref[...], preferred_element_type=F32).astype(BF)

    row_band = (_iota((2 * QROWS, KROWS), 0) % QROWS) // TOK
    col_band = _iota((2 * QROWS, KROWS), 1) // TOK
    bias = jnp.where((row_band == place_ref[0]) & (col_band == band), FAR, 0.0).astype(F32)

    lane = _iota((QROWS, LANES), 1) % SLOT
    own_lane = _iota((TOK, LANES), 1) % SLOT
    logs = jnp.zeros((QROWS, LANES), F32)
    own_logs = jnp.zeros((TOK, LANES), F32)
    for pair in range(HEADS // 2):
        cut = slice(pair * LANES, (pair + 1) * LANES)
        mixed, low, high = _attend(queries[:, cut], keys[:, cut], values[:, cut], bias)
        part_ref[:, :, cut] = mixed.astype(BF).reshape(NQ, TOK, LANES)
        logs = jnp.where(lane == 2 * pair, low, jnp.where(lane == 2 * pair + 1, high, logs))
        mixed, low, high = _attend(
            queries[pl.ds(mine, TOK), cut], fresh_keys[:, cut], fresh_values[:, cut], None
        )
        own_ref[:, cut] = mixed.astype(BF)
        own_logs = jnp.where(own_lane == 2 * pair, low, jnp.where(own_lane == 2 * pair + 1, high, own_logs))
    part_ref[:, :, C:] = _pack_logs(logs).reshape(NQ, TOK, LANES)
    own_ref[:, C:] = _pack_logs(own_logs)


def merge_kernel(part_ref, own_ref, projected_ref, latent_ref, output_ref, level_ref):
    slot = _iota((LANES, C), 0)
    head = _iota((LANES, C), 1) // HEAD
    spread = jnp.where((slot % SLOT == head) & (slot < 3 * SLOT), 1.0, 0.0).astype(BF)
    logs = jnp.dot(part_ref[:, :, C:].reshape(QROWS, LANES), spread, preferred_element_type=F32)
    logs = logs.reshape(NQ, TOK, C)
    own_logs = jnp.dot(own_ref[:, C:], spread, preferred_element_type=F32)
    top = jnp.maximum(jnp.max(logs, axis=0), own_logs)
    weight = jnp.exp2(own_logs - top)
    total = weight
    mixed = weight * own_ref[:, :C].astype(F32)
    for index in range(NQ):
        weight = jnp.exp2(logs[index] - top)
        total = total + weight
        mixed = mixed + weight * part_ref[index, :, :C].astype(F32)
    attended = (mixed / total).astype(BF)
    out = jnp.dot(attended, output_ref[...], preferred_element_type=F32)
    level = latent_ref[...].reshape(TOK, C).astype(F32) + projected_ref[...] + out
    level_ref[...] = level.astype(BF).reshape(1, TOK, C)


def _call(kernel, out_shape, n_in, scalar=False, scratch=(), limit=32 * 2**20):
    specs = [pl.BlockSpec(memory_space=pltpu.VMEM)] * n_in
    if scalar:
        specs = [pl.BlockSpec(memory_space=pltpu.SMEM)] + specs[1:]
    several = isinstance(out_shape, tuple)
    whole = pl.BlockSpec(memory_space=pltpu.VMEM)
    return pl.pallas_call(
        kernel,
        out_shape=out_shape,
        in_specs=specs,
        out_specs=(whole,) * len(out_shape) if several else whole,
        scratch_shapes=list(scratch),
        compiler_params=pltpu.CompilerParams(vmem_limit_bytes=limit),
    )


def _share(block, groups):
    copies = jnp.broadcast_to(block[None], (len(groups[0]),) + block.shape)
    return lax.all_to_all(copies, "patch", 0, 0, axis_index_groups=groups)


def on_device(latent, stale_hidden, input_proj, query_proj, key_proj, value_proj, output_proj):
    me = lax.axis_index("patch")
    y, x, z = me // 16, (me // 4) % 4, me % 4
    corner = (y % 2) * 4 + (x % 2) * 2 + z % 2
    cube = (y // 2) * 4 + (x // 2) * 2 + z // 2
    place = jnp.stack([corner, cube]).astype(jnp.int32)

    shape = jax.ShapeDtypeStruct
    stale = _share(stale_hidden, CORNERS)
    latents = _share(latent.reshape(TOK, C), CUBES)
    stats = _call(stats_kernel, shape((2, C), F32), 1)(latents)
    stats = _share(stats, CORNERS)
    parts, own, projected, next_hidden = _call(
        main_kernel,
        (shape((NQ, TOK, WIDE), BF), shape((TOK, WIDE), BF), shape((TOK, C), F32), shape((TOK, C), BF)),
        8,
        scalar=True,
        scratch=(pltpu.VMEM((QROWS, C), F32), pltpu.VMEM((QROWS, C), BF), pltpu.VMEM((QROWS, C), BF)),
    )(place, latents, stats, stale, input_proj, query_proj, key_proj, value_proj)
    parts = lax.all_to_all(parts, "patch", 0, 0, axis_index_groups=CUBES)
    level_out = _call(merge_kernel, shape((1, TOK, C), BF), 5)(parts, own, projected, latent, output_proj)
    return level_out, next_hidden


def solution(mesh):
    rows = P(("batch", "patch"), None)
    return jax.shard_map(
        on_device,
        mesh=mesh,
        in_specs=(P(("batch", "patch"), None, None), rows, P(), P(), P(), P(), P()),
        out_specs=(P(("batch", "patch"), None, None), rows),
        check_vma=False,
    )
```

time: 801 us -> 82.2 us (0.10)
  the two profiles are of different devices: /device:TPU:64 before, /device:TPU:16 now
where the time goes in v1:
time: 82.2 us; the launch traced here: 81.7 us
  blocking collectives  45 us (55%)
  waiting for transfers between devices  19.3 us (23%)
  Pallas kernels  7.65 us (9%)
  starting transfers between devices  6.05 us (7%)
  local copies, waits for them, and re-layouts  2.88 us (4%)
    all_to_all x2, blocking collectives, _share(): return lax.all_to_all(copies, 'patch', 0, 0, axis_index_groups=groups)  35.1 us
    all_to_all x1, waiting for transfers between devices, _share(): return lax.all_to_all(copies, 'patch', 0, 0, axis_index_groups=groups)  19.3 us
    all_to_all x1, blocking collectives, on_device(): parts = lax.all_to_all(parts, 'patch', 0, 0, axis_index_groups=CUBES)  9.89 us
    pallas_call x1, Pallas kernels, on_device(): _call(main_kernel, (shape((NQ, TOK, WIDE), BF), shape((TOK, WIDE), BF), s...  6.31 us
    all_to_all x1, starting transfers between devices, _share(): return lax.all_to_all(copies, 'patch', 0, 0, axis_index_groups=groups)  6.05 us
    broadcast_in_dim x3, local copies, waits for them, and re-layouts, _share(): copies = jnp.broadcast_to(block[None], (len(groups[0]),) + block.shape)  1.72 us
  transfers between devices with their start and end apart: 1, of which 1 were waited for; matrix products, arithmetic and copies ran while one was open for 0% of the time, Pallas kernels for 0%

profile of v1, /device:TPU:16, one launch (start us, length us, event | category | flops | bytes accessed | tf_op | source)
XLA Modules:
  0.0 81.7 jit_solution(15754396261715386109)
XLA Ops:
  0.6 0.8 broadcast_in_dim.9
  1.4 13.0 %all_to_all.20.latent_ref = bf16[8,32,640]{2,1,0:T(8,128)(2,1)S(1)} all-to-all(bf16[8,32,640]{2,1,0:T(8,128)(2,1)S(1)} %broadcast_in_dim.9), channel_id=1, replica_groups={{0,1,4,5,16,17,20,21},{2,3,6,7,18,19,22,23},{8,9,12,13,24,25,28,29},{10..., dimensions={0} | all-to-all | bytes 655360 | tf_op jit(solution)/shard_map/all_to_all | solution.py:206
  14.4 0.0 copy-start.6
  14.4 0.2 shard_map.86
  14.6 0.0 copy-start.2
  14.6 22.2 %all_to_all.21.stats_ref = f32[16,2,640]{2,1,0:T(2,128)S(1)} all-to-all(f32[16,2,640]{2,1,0:T(2,128)S(1)} %broadcast_in_dim.10), channel_id=1, replica_groups={{0,2,8,10,32,34,40,42,64,66,72,74,96,98,104,106},{1,3,9,11,33,35,41,43,..., dimensions={0} | all-to-all | bytes 163840 | tf_op jit(solution)/shard_map/all_to_all | solution.py:206
  36.8 0.0 copy-done.6
  36.8 0.0 copy-start.1
  36.8 0.9 %broadcast_in_dim.22 = bf16[16,32,640]{2,1,0:T(8,128)(2,1)} broadcast(bf16[32,640]{1,0:T(8,128)(2,1)S(1)} %copy-done.6), dimensions={1,2} | broadcast | bytes 696320 | tf_op jit(solution)/shard_map/broadcast_in_dim | solution.py:205
  37.7 0.0 copy-start
  37.7 6.1 %all-to-all-start.2 = ((bf16[16,32,640]{2,1,0:T(8,128)(2,1)}), bf16[16,32,640]{2,1,0:T(8,128)(2,1)S(1)}, u32[]{:S(2)}, u32[]{:S(2)}) async-start(bf16[16,32,640]{2,1,0:T(8,128)(2,1)} %broadcast_in_dim.22), calls=%async_computation.2 | async-start | bytes 1310720 | tf_op jit(solution)/shard_map/all_to_all | solution.py:206
  43.7 0.1 pad_add_fusion.place_ref
  43.8 19.3 %all-to-all-done.2.stale_ref = bf16[16,32,640]{2,1,0:T(8,128)(2,1)S(1)} async-done(((bf16[16,32,640]{2,1,0:T(8,128)(2,1)}), bf16[16,32,640]{2,1,0:T(8,128)(2,1)S(1)}, u32[]{:S(2)}, u32[]{:S(2)}) %all-to-all-start.2) | async-done | bytes 655392 | tf_op jit(solution)/shard_map/all_to_all | solution.py:206
  63.1 0.0 copy-done.2
  63.2 0.0 copy-done.1
  63.2 0.0 copy-done
  63.2 0.0 copy-start.3
  63.2 1.1 %copy-done.3 = bf16[640,640]{1,0:T(8,128)(2,1)S(1)} copy-done((bf16[640,640]{1,0:T(8,128)(2,1)S(1)}, bf16[640,640]{1,0:T(8,128)(2,1)}, u32[]{:S(2)}) %copy-start.3) | copy-done | bytes 819224
  64.3 6.3 %shard_map.87 = (bf16[8,32,768]{2,1,0:T(8,128)(2,1)S(1)}, bf16[32,768]{1,0:T(8,128)(2,1)S(1)}, f32[32,640]{1,0:T(8,128)S(1)}, bf16[32,640]{1,0:T(8,128)(2,1)}) custom-call(s32[2]{0:T(128)S(1)} %pad_add_fusion.place_ref, bf16[8,32,640]{2,1,0:T(8,128)(2,1)S(1)} %all_to_all.20.latent_ref, f32[16,2,640]{2,1,0:T(2,128)S(1)} %all_to_all.21.stats_ref, ...), custom_call_target="tpu_custom_call" | custom-call | tf_op jit(solution)/shard_map/pallas_call | solution.py:221
  70.6 0.0 copy-start.5
  70.6 9.9 %all_to_all.22.part_ref = bf16[8,32,768]{2,1,0:T(8,128)(2,1)S(1)} all-to-all(bf16[8,32,768]{2,1,0:T(8,128)(2,1)S(1)} %get-tuple-element.6), channel_id=1, replica_groups={{0,1,4,5,16,17,20,21},{2,3,6,7,18,19,22,23},{8,9,12,13,24,25,28,29},{10..., dimensions={0} | all-to-all | bytes 786432 | tf_op jit(solution)/shard_map/all_to_all | solution.py:228
  80.5 0.0 copy-done.4
  80.5 0.0 copy-done.5
  80.5 1.2 %shard_map.88 = bf16[1,32,640]{2,1,0:T(8,128)(2,1)} custom-call(bf16[8,32,768]{2,1,0:T(8,128)(2,1)S(1)} %all_to_all.22.part_ref, bf16[32,768]{1,0:T(8,128)(2,1)S(1)} %get-tuple-element.7.own_ref, f32[32,640]{1,0:T(8,128)S(1)} %get-tuple-element.8.projected_ref, bf16[1,32,640]{2,1,0:T(8,128)(2,1)S(1)} %copy-done.5, bf16[640,640]{1,0:T(8,128)(2,1)S(1)} %copy-done.4), custom_call_target="tpu_custom_call" | custom-call | tf_op jit(solution)/shard_map/pallas_call | solution.py:229
  (2 shorter events, 0.0 us)
Async XLA Ops:
  14.4 22.4 %copy-start.6 = (bf16[32,640]{1,0:T(8,128)(2,1)S(1)}, bf16[32,640]{1,0:T(8,128)(2,1)}, u32[]{:S(2)}) copy-start(bf16[32,640]{1,0:T(8,128)(2,1)} %param.8) | copy-start | bytes 122884
  14.6 48.6 %copy-start.2 = (bf16[640,640]{1,0:T(8,128)(2,1)S(1)}, bf16[640,640]{1,0:T(8,128)(2,1)}, u32[]{:S(2)}) copy-start(bf16[640,640]{1,0:T(8,128)(2,1)} %key_ref.1) | copy-start | bytes 2457604
  36.8 26.4 %copy-start.1 = (bf16[640,640]{1,0:T(8,128)(2,1)S(1)}, bf16[640,640]{1,0:T(8,128)(2,1)}, u32[]{:S(2)}) copy-start(bf16[640,640]{1,0:T(8,128)(2,1)} %query_ref.1) | copy-start | bytes 2457604
  37.7 25.5 %copy-start = (bf16[640,640]{1,0:T(8,128)(2,1)S(1)}, bf16[640,640]{1,0:T(8,128)(2,1)}, u32[]{:S(2)}) copy-start(bf16[640,640]{1,0:T(8,128)(2,1)} %input_ref.1) | copy-start | bytes 2457604
  37.7 25.5 %all-to-all-start.2 = ((bf16[16,32,640]{2,1,0:T(8,128)(2,1)}), bf16[16,32,640]{2,1,0:T(8,128)(2,1)S(1)}, u32[]{:S(2)}, u32[]{:S(2)}) async-start(bf16[16,32,640]{2,1,0:T(8,128)(2,1)} %broadcast_in_dim.22), calls=%async_computation.2 | async-start | bytes 1310720 | tf_op jit(solution)/shard_map/all_to_all | solution.py:206
  63.2 1.1 %copy-start.3 = (bf16[640,640]{1,0:T(8,128)(2,1)S(1)}, bf16[640,640]{1,0:T(8,128)(2,1)}, u32[]{:S(2)}) copy-start(bf16[640,640]{1,0:T(8,128)(2,1)} %value_ref.1) | copy-start | bytes 2457604
  64.3 16.2 %copy-start.4 = (bf16[640,640]{1,0:T(8,128)(2,1)S(1)}, bf16[640,640]{1,0:T(8,128)(2,1)}, u32[]{:S(2)}) copy-start(bf16[640,640]{1,0:T(8,128)(2,1)} %output_ref.1) | copy-start | bytes 2457604
  70.6 9.9 %copy-start.5 = (bf16[1,32,640]{2,1,0:T(8,128)(2,1)S(1)}, bf16[1,32,640]{2,1,0:T(8,128)(2,1)}, u32[]{:S(2)}) copy-start(bf16[1,32,640]{2,1,0:T(8,128)(2,1)} %latent_ref.1) | copy-start | bytes 122884

commit v2 on v1

--- a/solution.py
+++ b/solution.py
@@ -16,6 +16,7 @@
 LANES = 128
 SLOT = 32
 WIDE = C + LANES
+STATS = TOK * C // LANES
 STEP = math.log2(math.e) / math.sqrt(HEAD)
 FAR = -1e30
 
@@ -50,20 +51,37 @@
     return first, second, rest - second
 
 
-def stats_kernel(latent_ref, out_ref):
+def _same_group(shape, channel_axis):
+    group_axis = 1 - channel_axis
+    return jnp.where((_iota(shape, channel_axis) * 52429) >> 20 == _iota(shape, group_axis), 1.0, 0.0).astype(BF)
+
+
+def _stack_pieces(*rows):
+    which = _iota((16, rows[0].shape[1]), 0)
+    stacked = jnp.zeros((16, rows[0].shape[1]), F32)
+    for index, piece in enumerate(p for row in rows for p in _pieces(row)):
+        stacked = jnp.where(which == index, piece, stacked)
+    return stacked.astype(BF)
+
+
+def pack_kernel(latent_ref, stale_ref, out_ref):
     cells = latent_ref[...].astype(F32).reshape(QROWS, C)
-    center = jnp.sum(cells, axis=0, keepdims=True) * (1.0 / QROWS)
-    away = jnp.sum(jnp.square(cells - center), axis=0, keepdims=True)
-    out_ref[0:1, :] = center
-    out_ref[1:2, :] = away
-
-
-def _group_mean(row, same_group):
-    first, second, third = _pieces(row)
-    which = _iota((16, C), 0)
-    stacked = jnp.where(which == 0, first, jnp.where(which == 1, second, jnp.where(which == 2, third, 0.0)))
-    sums = jnp.dot(stacked.astype(BF), same_group, preferred_element_type=F32)
-    return jnp.sum(sums, axis=0, keepdims=True) * (1.0 / GROUP)
+    to_group = _same_group((C, LANES), 0)
+    to_channel = _same_group((LANES, C), 1)
+
+    def group_sums(row):
+        sums = jnp.dot(_stack_pieces(row), to_group, preferred_element_type=F32)
+        return jnp.sum(sums, axis=0, keepdims=True)
+
+    center = group_sums(jnp.sum(cells, axis=0, keepdims=True)) * (1.0 / (QROWS * GROUP))
+    centers = jnp.dot(_stack_pieces(center), to_channel, preferred_element_type=F32)
+    shifted = cells - jnp.sum(centers, axis=0, keepdims=True)
+    away = group_sums(jnp.sum(jnp.square(shifted), axis=0, keepdims=True))
+    stats = _stack_pieces(center, away)
+    for index in range(NK):
+        for part in range(C // LANES):
+            out_ref[index, part * TOK : (part + 1) * TOK, :] = stale_ref[:, part * LANES : (part + 1) * LANES]
+        out_ref[index, STATS:, :] = stats
 
 
 def _attend(q_pair, k_pair, v_pair, bias):
@@ -93,8 +111,7 @@
 def main_kernel(
     place_ref,
     latent_ref,
-    stats_ref,
-    stale_ref,
+    block_ref,
     input_ref,
     query_ref,
     key_ref,
@@ -110,17 +127,20 @@
     mine = pl.multiple_of(place_ref[0] * TOK, TOK)
     band = place_ref[1]
 
-    stats = stats_ref[...]
-    parts_mean = stats[:, 0, :]
-    parts_away = stats[:, 1, :]
+    stats = block_ref[:, STATS:, :].reshape(NK * 16, LANES)
+    target = _iota((2 * NK, NK * 16), 0)
+    source = _iota((2 * NK, NK * 16), 1) - (target % NK) * 16 - (target // NK) * 3
+    picked = jnp.where((source >= 0) & (source < 3), 1.0, 0.0).astype(BF)
+    stats = jnp.dot(picked, stats, preferred_element_type=F32)
+    parts_mean, parts_away = stats[:NK], stats[NK:]
     mean = jnp.sum(parts_mean, axis=0, keepdims=True) * (1.0 / NK)
-    away = jnp.sum(parts_away + float(QROWS) * jnp.square(parts_mean - mean), axis=0, keepdims=True)
-    row_group = (_iota((C, C), 0) * 52429) >> 20
-    col_group = (_iota((C, C), 1) * 52429) >> 20
-    same_group = jnp.where(row_group == col_group, 1.0, 0.0).astype(BF)
-    center = _group_mean(mean, same_group)
-    spread = _group_mean(away * (1.0 / (QROWS * NK)) + jnp.square(mean - center), same_group)
-    gain = lax.rsqrt(spread + 1e-06)
+    cell_count = float(QROWS * GROUP)
+    away = jnp.sum(parts_away + cell_count * jnp.square(parts_mean - mean), axis=0, keepdims=True)
+    gain = lax.rsqrt(away * (1.0 / (cell_count * NK)) + 1e-06)
+    spread = jnp.dot(_stack_pieces(mean, gain), _same_group((LANES, C), 1), preferred_element_type=F32)
+    which = _iota((16, C), 0)
+    center = jnp.sum(jnp.where(which < 3, spread, 0.0), axis=0, keepdims=True)
+    gain = jnp.sum(jnp.where(which < 3, 0.0, spread), axis=0, keepdims=True)
     cells = latent_ref[...].astype(F32).reshape(QROWS, C)
     normed = ((cells - center) * gain).astype(BF)
 
@@ -136,7 +156,9 @@
     hidden_ref[...] = own_hidden
     queries[...] = jnp.dot(hidden, query_ref[...], preferred_element_type=F32).astype(BF)
 
-    stale = stale_ref[...].reshape(KROWS, C)
+    stale = jnp.concatenate(
+        [block_ref[:, part * TOK : (part + 1) * TOK, :].reshape(KROWS, LANES) for part in range(C // LANES)], axis=1
+    )
     keys = jnp.dot(stale, key_ref[...], preferred_element_type=F32).astype(BF)
     values = jnp.dot(stale, value_ref[...], preferred_element_type=F32).astype(BF)
     fresh_keys = jnp.dot(own_hidden, key_ref[...], preferred_element_type=F32).astype(BF)
@@ -214,17 +236,16 @@
     place = jnp.stack([corner, cube]).astype(jnp.int32)
 
     shape = jax.ShapeDtypeStruct
-    stale = _share(stale_hidden, CORNERS)
     latents = _share(latent.reshape(TOK, C), CUBES)
-    stats = _call(stats_kernel, shape((2, C), F32), 1)(latents)
-    stats = _share(stats, CORNERS)
+    blocks = _call(pack_kernel, shape((NK, STATS + 16, LANES), BF), 2)(latents, stale_hidden)
+    blocks = lax.all_to_all(blocks, "patch", 0, 0, axis_index_groups=CORNERS)
     parts, own, projected, next_hidden = _call(
         main_kernel,
         (shape((NQ, TOK, WIDE), BF), shape((TOK, WIDE), BF), shape((TOK, C), F32), shape((TOK, C), BF)),
-        8,
+        7,
         scalar=True,
         scratch=(pltpu.VMEM((QROWS, C), F32), pltpu.VMEM((QROWS, C), BF), pltpu.VMEM((QROWS, C), BF)),
-    )(place, latents, stats, stale, input_proj, query_proj, key_proj, value_proj)
+    )(place, latents, blocks, input_proj, query_proj, key_proj, value_proj)
     parts = lax.all_to_all(parts, "patch", 0, 0, axis_index_groups=CUBES)
     level_out = _call(merge_kernel, shape((1, TOK, C), BF), 5)(parts, own, projected, latent, output_proj)
     return level_out, next_hidden

time: 82.2 us -> 70.4 us (0.86)
  the two profiles are of different devices: /device:TPU:16 before, /device:TPU:8 now
where the time goes in v2:
time: 70.4 us; the launch traced here: 69.9 us
  blocking collectives  27.7 us (39%)
  waiting for transfers between devices  20.2 us (29%)
  starting transfers between devices  10.2 us (14%)
  Pallas kernels  8.86 us (13%)
  local copies, waits for them, and re-layouts  1.97 us (3%)
  between operations  0.81 us (1%)
    all_to_all x1, waiting for transfers between devices, on_device(): blocks = lax.all_to_all(blocks, 'patch', 0, 0, axis_index_groups=CORNERS)  20.2 us
    all_to_all x1, blocking collectives, _share(): return lax.all_to_all(copies, 'patch', 0, 0, axis_index_groups=groups)  14.1 us
    all_to_all x1, blocking collectives, on_device(): parts = lax.all_to_all(parts, 'patch', 0, 0, axis_index_groups=CUBES)  13.7 us
    all_to_all x1, starting transfers between devices, on_device(): blocks = lax.all_to_all(blocks, 'patch', 0, 0, axis_index_groups=CORNERS)  10.2 us
    pallas_call x1, Pallas kernels, on_device(): _call(main_kernel, (shape((NQ, TOK, WIDE), BF), shape((TOK, WIDE), BF), s...  6.13 us
    pallas_call x1, Pallas kernels, on_device(): _call(pack_kernel, shape((NK, STATS + 16, LANES), BF), 2)  1.53 us
  transfers between devices with their start and end apart: 1, of which 1 were waited for; matrix products, arithmetic and copies ran while one was open for 0% of the time, Pallas kernels for 0%

profile of v2, /device:TPU:8, one launch (start us, length us, event | category | flops | bytes accessed | tf_op | source)
XLA Modules:
  0.0 69.9 jit_solution(11786481443685162481)
XLA Ops:
  0.6 0.8 %broadcast_in_dim.8 = bf16[8,32,640]{2,1,0:T(8,128)(2,1)S(1)} broadcast(bf16[32,640]{1,0:T(8,128)(2,1)} %bitcast.3), dimensions={1,2} | broadcast | bytes 368640 | tf_op jit(solution)/shard_map/broadcast_in_dim | solution.py:227
  1.4 0.0 copy-start.6
  1.5 14.1 %all_to_all.15.latent_ref = bf16[8,32,640]{2,1,0:T(8,128)(2,1)S(1)} all-to-all(bf16[8,32,640]{2,1,0:T(8,128)(2,1)S(1)} %broadcast_in_dim.8), channel_id=1, replica_groups={{0,1,4,5,16,17,20,21},{2,3,6,7,18,19,22,23},{8,9,12,13,24,25,28,29},{10..., dimensions={0} | all-to-all | bytes 655360 | tf_op jit(solution)/shard_map/all_to_all | solution.py:228
  15.5 0.0 copy-done.6
  15.5 0.0 copy-start.3
  15.5 1.5 %shard_map.86 = bf16[16,176,128]{2,1,0:T(8,128)(2,1)} custom-call(bf16[8,32,640]{2,1,0:T(8,128)(2,1)S(1)} %all_to_all.15.latent_ref, bf16[32,640]{1,0:T(8,128)(2,1)S(1)} %copy-done.6), custom_call_target="tpu_custom_call" | custom-call | tf_op jit(solution)/shard_map/pallas_call | solution.py:240
  17.0 0.0 copy-start.1
  17.0 0.0 copy-start.2
  17.0 10.2 %all-to-all-start.1 = ((bf16[16,176,128]{2,1,0:T(8,128)(2,1)}), bf16[16,176,128]{2,1,0:T(8,128)(2,1)S(1)}, u32[]{:S(2)}, u32[]{:S(2)}) async-start(bf16[16,176,128]{2,1,0:T(8,128)(2,1)} %shard_map.86), calls=%async_computation.1 | async-start | bytes 1441792 | tf_op jit(solution)/shard_map/all_to_all | solution.py:241
  27.4 0.1 pad_add_fusion.place_ref
  27.5 20.2 %all-to-all-done.1.block_ref = bf16[16,176,128]{2,1,0:T(8,128)(2,1)S(1)} async-done(((bf16[16,176,128]{2,1,0:T(8,128)(2,1)}), bf16[16,176,128]{2,1,0:T(8,128)(2,1)S(1)}, u32[]{:S(2)}, u32[]{:S(2)}) %all-to-all-start.1) | async-done | bytes 720928 | tf_op jit(solution)/shard_map/all_to_all | solution.py:241
  47.7 0.0 copy-done.3
  47.7 0.0 copy-done.1
  47.7 0.0 copy-done.2
  47.7 0.0 copy-start.4
  47.7 1.1 %copy-done.4 = bf16[640,640]{1,0:T(8,128)(2,1)S(1)} copy-done((bf16[640,640]{1,0:T(8,128)(2,1)S(1)}, bf16[640,640]{1,0:T(8,128)(2,1)}, u32[]{:S(2)}) %copy-start.4) | copy-done | bytes 819224
  48.9 0.0 copy-start
  48.9 6.1 %shard_map.87 = (bf16[8,32,768]{2,1,0:T(8,128)(2,1)S(1)}, bf16[32,768]{1,0:T(8,128)(2,1)S(1)}, f32[32,640]{1,0:T(8,128)S(1)}, bf16[32,640]{1,0:T(8,128)(2,1)}) custom-call(s32[2]{0:T(128)S(1)} %pad_add_fusion.place_ref, bf16[8,32,640]{2,1,0:T(8,128)(2,1)S(1)} %all_to_all.15.latent_ref, bf16[16,176,128]{2,1,0:T(8,128)(2,1)S(1)} %all-to-all-done.1.block_ref, ...), custom_call_target="tpu_custom_call" | custom-call | tf_op jit(solution)/shard_map/pallas_call | solution.py:242
  55.0 0.0 copy-start.5
  55.0 13.7 %all_to_all.16.part_ref = bf16[8,32,768]{2,1,0:T(8,128)(2,1)S(1)} all-to-all(bf16[8,32,768]{2,1,0:T(8,128)(2,1)S(1)} %get-tuple-element.6), channel_id=1, replica_groups={{0,1,4,5,16,17,20,21},{2,3,6,7,18,19,22,23},{8,9,12,13,24,25,28,29},{10..., dimensions={0} | all-to-all | bytes 786432 | tf_op jit(solution)/shard_map/all_to_all | solution.py:249
  68.7 0.0 copy-done
  68.7 0.0 copy-done.5
  68.7 1.2 %shard_map.88 = bf16[1,32,640]{2,1,0:T(8,128)(2,1)} custom-call(bf16[8,32,768]{2,1,0:T(8,128)(2,1)S(1)} %all_to_all.16.part_ref, bf16[32,768]{1,0:T(8,128)(2,1)S(1)} %get-tuple-element.7.own_ref, f32[32,640]{1,0:T(8,128)S(1)} %get-tuple-element.8.projected_ref, bf16[1,32,640]{2,1,0:T(8,128)(2,1)S(1)} %copy-done.5, bf16[640,640]{1,0:T(8,128)(2,1)S(1)} %copy-done), custom_call_target="tpu_custom_call" | custom-call | tf_op jit(solution)/shard_map/pallas_call | solution.py:250
Async XLA Ops:
  1.4 14.1 %copy-start.6 = (bf16[32,640]{1,0:T(8,128)(2,1)S(1)}, bf16[32,640]{1,0:T(8,128)(2,1)}, u32[]{:S(2)}) copy-start(bf16[32,640]{1,0:T(8,128)(2,1)} %stale_ref.1) | copy-start | bytes 122884
  15.5 32.2 %copy-start.3 = (bf16[640,640]{1,0:T(8,128)(2,1)S(1)}, bf16[640,640]{1,0:T(8,128)(2,1)}, u32[]{:S(2)}) copy-start(bf16[640,640]{1,0:T(8,128)(2,1)} %key_ref.1) | copy-start | bytes 2457604
  17.0 30.7 %copy-start.1 = (bf16[640,640]{1,0:T(8,128)(2,1)S(1)}, bf16[640,640]{1,0:T(8,128)(2,1)}, u32[]{:S(2)}) copy-start(bf16[640,640]{1,0:T(8,128)(2,1)} %input_ref.1) | copy-start | bytes 2457604
  17.0 30.7 %copy-start.2 = (bf16[640,640]{1,0:T(8,128)(2,1)S(1)}, bf16[640,640]{1,0:T(8,128)(2,1)}, u32[]{:S(2)}) copy-start(bf16[640,640]{1,0:T(8,128)(2,1)} %query_ref.1) | copy-start | bytes 2457604
  17.0 30.7 %all-to-all-start.1 = ((bf16[16,176,128]{2,1,0:T(8,128)(2,1)}), bf16[16,176,128]{2,1,0:T(8,128)(2,1)S(1)}, u32[]{:S(2)}, u32[]{:S(2)}) async-start(bf16[16,176,128]{2,1,0:T(8,128)(2,1)} %shard_map.86), calls=%async_computation.1 | async-start | bytes 1441792 | tf_op jit(solution)/shard_map/all_to_all | solution.py:241
  47.7 1.1 %copy-start.4 = (bf16[640,640]{1,0:T(8,128)(2,1)S(1)}, bf16[640,640]{1,0:T(8,128)(2,1)}, u32[]{:S(2)}) copy-start(bf16[640,640]{1,0:T(8,128)(2,1)} %value_ref.1) | copy-start | bytes 2457604
  48.9 19.8 %copy-start = (bf16[640,640]{1,0:T(8,128)(2,1)S(1)}, bf16[640,640]{1,0:T(8,128)(2,1)}, u32[]{:S(2)}) copy-start(bf16[640,640]{1,0:T(8,128)(2,1)} %output_ref.1) | copy-start | bytes 2457604
  55.0 13.7 %copy-start.5 = (bf16[1,32,640]{2,1,0:T(8,128)(2,1)S(1)}, bf16[1,32,640]{2,1,0:T(8,128)(2,1)}, u32[]{:S(2)}) copy-start(bf16[1,32,640]{2,1,0:T(8,128)(2,1)} %latent_ref.1) | copy-start | bytes 122884

commit v3 on v2

--- a/solution.py
+++ b/solution.py
@@ -30,10 +30,10 @@
     return [members[k] for k in sorted(members)]
 
 
-CUBES = _groups(lambda y, x, z: (y // 2, x // 2, z // 2))
-CORNERS = _groups(lambda y, x, z: (y % 2, x % 2, z % 2))
-NQ = len(CUBES[0])
-NK = len(CORNERS[0])
+BRICKS = _groups(lambda y, x, z: (y // 2, z // 2))
+SEATS = _groups(lambda y, x, z: (y % 2, x, z % 2))
+NQ = len(BRICKS[0])
+NK = len(SEATS[0])
 QROWS = NQ * TOK
 KROWS = NK * TOK
 BF = jnp.bfloat16
@@ -207,7 +207,7 @@
     level_ref[...] = level.astype(BF).reshape(1, TOK, C)
 
 
-def _call(kernel, out_shape, n_in, scalar=False, scratch=(), limit=32 * 2**20):
+def _call(kernel, out_shape, n_in, scalar=False, scratch=(), limit=16 * 2**20):
     specs = [pl.BlockSpec(memory_space=pltpu.VMEM)] * n_in
     if scalar:
         specs = [pl.BlockSpec(memory_space=pltpu.SMEM)] + specs[1:]
@@ -231,14 +231,12 @@
 def on_device(latent, stale_hidden, input_proj, query_proj, key_proj, value_proj, output_proj):
     me = lax.axis_index("patch")
     y, x, z = me // 16, (me // 4) % 4, me % 4
-    corner = (y % 2) * 4 + (x % 2) * 2 + z % 2
-    cube = (y // 2) * 4 + (x // 2) * 2 + z // 2
-    place = jnp.stack([corner, cube]).astype(jnp.int32)
+    place = jnp.stack([(y % 2) * 8 + x * 2 + z % 2, (y // 2) * 2 + z // 2]).astype(jnp.int32)
 
     shape = jax.ShapeDtypeStruct
-    latents = _share(latent.reshape(TOK, C), CUBES)
+    latents = _share(latent.reshape(TOK, C), BRICKS)
     blocks = _call(pack_kernel, shape((NK, STATS + 16, LANES), BF), 2)(latents, stale_hidden)
-    blocks = lax.all_to_all(blocks, "patch", 0, 0, axis_index_groups=CORNERS)
+    blocks = lax.all_to_all(blocks, "patch", 0, 0, axis_index_groups=SEATS)
     parts, own, projected, next_hidden = _call(
         main_kernel,
         (shape((NQ, TOK, WIDE), BF), shape((TOK, WIDE), BF), shape((TOK, C), F32), shape((TOK, C), BF)),
@@ -246,7 +244,7 @@
         scalar=True,
         scratch=(pltpu.VMEM((QROWS, C), F32), pltpu.VMEM((QROWS, C), BF), pltpu.VMEM((QROWS, C), BF)),
     )(place, latents, blocks, input_proj, query_proj, key_proj, value_proj)
-    parts = lax.all_to_all(parts, "patch", 0, 0, axis_index_groups=CUBES)
+    parts = lax.all_to_all(parts, "patch", 0, 0, axis_index_groups=BRICKS)
     level_out = _call(merge_kernel, shape((1, TOK, C), BF), 5)(parts, own, projected, latent, output_proj)
     return level_out, next_hidden
 

time: 70.4 us -> 69.1 us (0.982)
  the two profiles are of different devices: /device:TPU:8 before, /device:TPU:1 now
where the time goes in v3:
time: 69.1 us; the launch traced here: 68.8 us
  blocking collectives  36.7 us (53%)
  starting transfers between devices  10.7 us (15%)
  waiting for transfers between devices  10.4 us (15%)
  Pallas kernels  8.25 us (12%)
  local copies, waits for them, and re-layouts  2 us (3%)
    all_to_all x1, blocking collectives, on_device(): parts = lax.all_to_all(parts, 'patch', 0, 0, axis_index_groups=BRICKS)  19 us
    all_to_all x1, blocking collectives, _share(): return lax.all_to_all(copies, 'patch', 0, 0, axis_index_groups=groups)  17.7 us
    all_to_all x1, starting transfers between devices, on_device(): blocks = lax.all_to_all(blocks, 'patch', 0, 0, axis_index_groups=SEATS)  10.7 us
    all_to_all x1, waiting for transfers between devices, on_device(): blocks = lax.all_to_all(blocks, 'patch', 0, 0, axis_index_groups=SEATS)  10.4 us
    pallas_call x1, Pallas kernels, on_device(): _call(main_kernel, (shape((NQ, TOK, WIDE), BF), shape((TOK, WIDE), BF), s...  5.28 us
    pallas_call x1, Pallas kernels, on_device(): _call(pack_kernel, shape((NK, STATS + 16, LANES), BF), 2)  1.58 us
    pallas_call x1, Pallas kernels, on_device(): _call(merge_kernel, shape((1, TOK, C), BF), 5)  1.39 us
  transfers between devices with their start and end apart: 1, of which 1 were waited for; matrix products, arithmetic and copies ran while one was open for 0% of the time, Pallas kernels for 0%

profile of v3, /device:TPU:1, one launch (start us, length us, event | category | flops | bytes accessed | tf_op | source)
XLA Modules:
  0.0 68.8 jit_solution(17502032260818423696)
XLA Ops:
  0.6 0.8 %broadcast_in_dim.8 = bf16[16,32,640]{2,1,0:T(8,128)(2,1)S(1)} broadcast(bf16[32,640]{1,0:T(8,128)(2,1)} %bitcast.3), dimensions={1,2} | broadcast | bytes 696320 | tf_op jit(solution)/shard_map/broadcast_in_dim | solution.py:227
  1.5 0.0 copy-start.6
  1.5 0.0 copy-start.3
  1.5 17.7 %all_to_all.15.latent_ref = bf16[16,32,640]{2,1,0:T(8,128)(2,1)S(1)} all-to-all(bf16[16,32,640]{2,1,0:T(8,128)(2,1)S(1)} %broadcast_in_dim.8), channel_id=1, replica_groups={{0,1,4,5,8,9,12,13,16,17,20,21,24,25,28,29},{2,3,6,7,10,11,14,15,18,19,..., dimensions={0} | all-to-all | bytes 1310720 | tf_op jit(solution)/shard_map/all_to_all | solution.py:228
  19.2 0.0 copy-done.6
  19.2 0.0 copy-start.1
  19.2 0.0 copy-start.2
  19.2 1.6 %shard_map.86 = bf16[8,176,128]{2,1,0:T(8,128)(2,1)} custom-call(bf16[16,32,640]{2,1,0:T(8,128)(2,1)S(1)} %all_to_all.15.latent_ref, bf16[32,640]{1,0:T(8,128)(2,1)S(1)} %copy-done.6), custom_call_target="tpu_custom_call" | custom-call | tf_op jit(solution)/shard_map/pallas_call | solution.py:238
  20.8 10.7 %all-to-all-start.1 = ((bf16[8,176,128]{2,1,0:T(8,128)(2,1)}), bf16[8,176,128]{2,1,0:T(8,128)(2,1)S(1)}, u32[]{:S(2)}, u32[]{:S(2)}) async-start(bf16[8,176,128]{2,1,0:T(8,128)(2,1)} %shard_map.86), calls=%async_computation.1 | async-start | bytes 720896 | tf_op jit(solution)/shard_map/all_to_all | solution.py:239
  31.4 0.1 pad_add_fusion.place_ref
  31.5 10.4 %all-to-all-done.1.block_ref = bf16[8,176,128]{2,1,0:T(8,128)(2,1)S(1)} async-done(((bf16[8,176,128]{2,1,0:T(8,128)(2,1)}), bf16[8,176,128]{2,1,0:T(8,128)(2,1)S(1)}, u32[]{:S(2)}, u32[]{:S(2)}) %all-to-all-start.1) | async-done | bytes 360480 | tf_op jit(solution)/shard_map/all_to_all | solution.py:239
  41.9 0.0 copy-done.3
  41.9 0.0 copy-done.1
  41.9 0.0 copy-done.2
  41.9 0.0 copy-start.4
  41.9 1.1 %copy-done.4 = bf16[640,640]{1,0:T(8,128)(2,1)S(1)} copy-done((bf16[640,640]{1,0:T(8,128)(2,1)S(1)}, bf16[640,640]{1,0:T(8,128)(2,1)}, u32[]{:S(2)}) %copy-start.4) | copy-done | bytes 819224
  43.0 5.3 %shard_map.87 = (bf16[16,32,768]{2,1,0:T(8,128)(2,1)S(1)}, bf16[32,768]{1,0:T(8,128)(2,1)S(1)}, f32[32,640]{1,0:T(8,128)S(1)}, bf16[32,640]{1,0:T(8,128)(2,1)}) custom-call(s32[2]{0:T(128)S(1)} %pad_add_fusion.place_ref, bf16[16,32,640]{2,1,0:T(8,128)(2,1)S(1)} %all_to_all.15.latent_ref, bf16[8,176,128]{2,1,0:T(8,128)(2,1)S(1)} %all-to-all-done.1.block_ref, ...), custom_call_target="tpu_custom_call" | custom-call | tf_op jit(solution)/shard_map/pallas_call | solution.py:240
  48.3 0.0 copy-start
  48.3 0.0 copy-start.5
  48.3 19.0 %all_to_all.16.part_ref = bf16[16,32,768]{2,1,0:T(8,128)(2,1)S(1)} all-to-all(bf16[16,32,768]{2,1,0:T(8,128)(2,1)S(1)} %get-tuple-element.6), channel_id=1, replica_groups={{0,1,4,5,8,9,12,13,16,17,20,21,24,25,28,29},{2,3,6,7,10,11,14,15,18,19,..., dimensions={0} | all-to-all | bytes 1572864 | tf_op jit(solution)/shard_map/all_to_all | solution.py:247
  67.4 0.0 copy-done
  67.4 0.0 copy-done.5
  67.4 1.4 %shard_map.88 = bf16[1,32,640]{2,1,0:T(8,128)(2,1)} custom-call(bf16[16,32,768]{2,1,0:T(8,128)(2,1)S(1)} %all_to_all.16.part_ref, bf16[32,768]{1,0:T(8,128)(2,1)S(1)} %get-tuple-element.7.own_ref, f32[32,640]{1,0:T(8,128)S(1)} %get-tuple-element.8.projected_ref, bf16[1,32,640]{2,1,0:T(8,128)(2,1)S(1)} %copy-done.5, bf16[640,640]{1,0:T(8,128)(2,1)S(1)} %copy-done), custom_call_target="tpu_custom_call" | custom-call | tf_op jit(solution)/shard_map/pallas_call | solution.py:248
Async XLA Ops:
  1.5 17.7 %copy-start.6 = (bf16[32,640]{1,0:T(8,128)(2,1)S(1)}, bf16[32,640]{1,0:T(8,128)(2,1)}, u32[]{:S(2)}) copy-start(bf16[32,640]{1,0:T(8,128)(2,1)} %stale_ref.1) | copy-start | bytes 122884
  1.5 40.4 %copy-start.3 = (bf16[640,640]{1,0:T(8,128)(2,1)S(1)}, bf16[640,640]{1,0:T(8,128)(2,1)}, u32[]{:S(2)}) copy-start(bf16[640,640]{1,0:T(8,128)(2,1)} %key_ref.1) | copy-start | bytes 2457604
  19.2 22.7 %copy-start.1 = (bf16[640,640]{1,0:T(8,128)(2,1)S(1)}, bf16[640,640]{1,0:T(8,128)(2,1)}, u32[]{:S(2)}) copy-start(bf16[640,640]{1,0:T(8,128)(2,1)} %input_ref.1) | copy-start | bytes 2457604
  19.2 22.7 %copy-start.2 = (bf16[640,640]{1,0:T(8,128)(2,1)S(1)}, bf16[640,640]{1,0:T(8,128)(2,1)}, u32[]{:S(2)}) copy-start(bf16[640,640]{1,0:T(8,128)(2,1)} %query_ref.1) | copy-start | bytes 2457604
  20.8 21.1 %all-to-all-start.1 = ((bf16[8,176,128]{2,1,0:T(8,128)(2,1)}), bf16[8,176,128]{2,1,0:T(8,128)(2,1)S(1)}, u32[]{:S(2)}, u32[]{:S(2)}) async-start(bf16[8,176,128]{2,1,0:T(8,128)(2,1)} %shard_map.86), calls=%async_computation.1 | async-start | bytes 720896 | tf_op jit(solution)/shard_map/all_to_all | solution.py:239
  41.9 1.1 %copy-start.4 = (bf16[640,640]{1,0:T(8,128)(2,1)S(1)}, bf16[640,640]{1,0:T(8,128)(2,1)}, u32[]{:S(2)}) copy-start(bf16[640,640]{1,0:T(8,128)(2,1)} %value_ref.1) | copy-start | bytes 2457604
  48.3 19.1 %copy-start = (bf16[640,640]{1,0:T(8,128)(2,1)S(1)}, bf16[640,640]{1,0:T(8,128)(2,1)}, u32[]{:S(2)}) copy-start(bf16[640,640]{1,0:T(8,128)(2,1)} %output_ref.1) | copy-start | bytes 2457604
  48.3 19.1 %copy-start.5 = (bf16[1,32,640]{2,1,0:T(8,128)(2,1)S(1)}, bf16[1,32,640]{2,1,0:T(8,128)(2,1)}, u32[]{:S(2)}) copy-start(bf16[1,32,640]{2,1,0:T(8,128)(2,1)} %latent_ref.1) | copy-start | bytes 122884

commit v4 on v3

--- a/solution.py
+++ b/solution.py
@@ -108,24 +108,20 @@
     return jnp.where(lane < SLOT, first, jnp.where(lane < 2 * SLOT, second, third)).astype(BF)
 
 
-def main_kernel(
-    place_ref,
-    latent_ref,
-    block_ref,
-    input_ref,
-    query_ref,
-    key_ref,
-    value_ref,
-    part_ref,
-    own_ref,
-    projected_ref,
-    hidden_ref,
-    projected_all,
-    hidden_all,
-    queries,
+def _seat():
+    me = lax.axis_index("patch")
+    return ((me >> 4) & 1) * 8 + ((me >> 2) & 3) * 2 + (me & 1)
+
+
+def _brick():
+    me = lax.axis_index("patch")
+    return (me >> 5) * 2 + ((me >> 1) & 1)
+
+
+def query_kernel(
+    latent_ref, block_ref, input_ref, query_ref, queries_ref, own_queries_ref, projected_ref, hidden_ref, projected_all, hidden_all
 ):
-    mine = pl.multiple_of(place_ref[0] * TOK, TOK)
-    band = place_ref[1]
+    mine = pl.multiple_of(_seat() * TOK, TOK)
 
     stats = block_ref[:, STATS:, :].reshape(NK * 16, LANES)
     target = _iota((2 * NK, NK * 16), 0)
@@ -151,22 +147,23 @@
     row_spread = jnp.mean(jnp.square(shifted), axis=1, keepdims=True)
     hidden = (shifted * lax.rsqrt(row_spread + 1e-05)).astype(BF)
     hidden_all[...] = hidden
+    queries_ref[...] = jnp.dot(hidden, query_ref[...], preferred_element_type=F32).astype(BF)
     projected_ref[...] = projected_all[pl.ds(mine, TOK), :]
-    own_hidden = hidden_all[pl.ds(mine, TOK), :]
-    hidden_ref[...] = own_hidden
-    queries[...] = jnp.dot(hidden, query_ref[...], preferred_element_type=F32).astype(BF)
-
-    stale = jnp.concatenate(
-        [block_ref[:, part * TOK : (part + 1) * TOK, :].reshape(KROWS, LANES) for part in range(C // LANES)], axis=1
-    )
-    keys = jnp.dot(stale, key_ref[...], preferred_element_type=F32).astype(BF)
-    values = jnp.dot(stale, value_ref[...], preferred_element_type=F32).astype(BF)
-    fresh_keys = jnp.dot(own_hidden, key_ref[...], preferred_element_type=F32).astype(BF)
-    fresh_values = jnp.dot(own_hidden, value_ref[...], preferred_element_type=F32).astype(BF)
+    hidden_ref[...] = hidden_all[pl.ds(mine, TOK), :]
+    own_queries_ref[...] = queries_ref[pl.ds(mine, TOK), :]
+
+
+def attend_kernel(queries_ref, own_queries_ref, hidden_ref, block_ref, key_ref, value_ref, part_ref, own_ref):
+    strips = [block_ref[:, part * TOK : (part + 1) * TOK, :].reshape(KROWS, LANES) for part in range(C // LANES)]
+    both_hidden = jnp.concatenate([jnp.concatenate(strips, axis=1), hidden_ref[...]], axis=0)
+    both_keys = jnp.dot(both_hidden, key_ref[...], preferred_element_type=F32).astype(BF)
+    both_values = jnp.dot(both_hidden, value_ref[...], preferred_element_type=F32).astype(BF)
+    keys, fresh_keys = both_keys[:KROWS], both_keys[KROWS:]
+    values, fresh_values = both_values[:KROWS], both_values[KROWS:]
 
     row_band = (_iota((2 * QROWS, KROWS), 0) % QROWS) // TOK
     col_band = _iota((2 * QROWS, KROWS), 1) // TOK
-    bias = jnp.where((row_band == place_ref[0]) & (col_band == band), FAR, 0.0).astype(F32)
+    bias = jnp.where((row_band == _seat()) & (col_band == _brick()), FAR, 0.0).astype(F32)
 
     lane = _iota((QROWS, LANES), 1) % SLOT
     own_lane = _iota((TOK, LANES), 1) % SLOT
@@ -174,11 +171,11 @@
     own_logs = jnp.zeros((TOK, LANES), F32)
     for pair in range(HEADS // 2):
         cut = slice(pair * LANES, (pair + 1) * LANES)
-        mixed, low, high = _attend(queries[:, cut], keys[:, cut], values[:, cut], bias)
+        mixed, low, high = _attend(queries_ref[:, cut], keys[:, cut], values[:, cut], bias)
         part_ref[:, :, cut] = mixed.astype(BF).reshape(NQ, TOK, LANES)
         logs = jnp.where(lane == 2 * pair, low, jnp.where(lane == 2 * pair + 1, high, logs))
         mixed, low, high = _attend(
-            queries[pl.ds(mine, TOK), cut], fresh_keys[:, cut], fresh_values[:, cut], None
+            own_queries_ref[:, cut], fresh_keys[:, cut], fresh_values[:, cut], None
         )
         own_ref[:, cut] = mixed.astype(BF)
         own_logs = jnp.where(own_lane == 2 * pair, low, jnp.where(own_lane == 2 * pair + 1, high, own_logs))
@@ -186,7 +183,8 @@
     own_ref[:, C:] = _pack_logs(own_logs)
 
 
-def merge_kernel(part_ref, own_ref, projected_ref, latent_ref, output_ref, level_ref):
+def merge_kernel(part_ref, own_ref, projected_ref, hidden_ref, latent_ref, output_ref, level_ref, next_ref):
+    next_ref[...] = hidden_ref[...]
     slot = _iota((LANES, C), 0)
     head = _iota((LANES, C), 1) // HEAD
     spread = jnp.where((slot % SLOT == head) & (slot < 3 * SLOT), 1.0, 0.0).astype(BF)
@@ -207,10 +205,8 @@
     level_ref[...] = level.astype(BF).reshape(1, TOK, C)
 
 
-def _call(kernel, out_shape, n_in, scalar=False, scratch=(), limit=16 * 2**20):
+def _call(kernel, out_shape, n_in, scratch=(), limit=16 * 2**20):
     specs = [pl.BlockSpec(memory_space=pltpu.VMEM)] * n_in
-    if scalar:
-        specs = [pl.BlockSpec(memory_space=pltpu.SMEM)] + specs[1:]
     several = isinstance(out_shape, tuple)
     whole = pl.BlockSpec(memory_space=pltpu.VMEM)
     return pl.pallas_call(
@@ -229,24 +225,23 @@
 
 
 def on_device(latent, stale_hidden, input_proj, query_proj, key_proj, value_proj, output_proj):
-    me = lax.axis_index("patch")
-    y, x, z = me // 16, (me // 4) % 4, me % 4
-    place = jnp.stack([(y % 2) * 8 + x * 2 + z % 2, (y // 2) * 2 + z // 2]).astype(jnp.int32)
-
     shape = jax.ShapeDtypeStruct
     latents = _share(latent.reshape(TOK, C), BRICKS)
     blocks = _call(pack_kernel, shape((NK, STATS + 16, LANES), BF), 2)(latents, stale_hidden)
     blocks = lax.all_to_all(blocks, "patch", 0, 0, axis_index_groups=SEATS)
-    parts, own, projected, next_hidden = _call(
-        main_kernel,
-        (shape((NQ, TOK, WIDE), BF), shape((TOK, WIDE), BF), shape((TOK, C), F32), shape((TOK, C), BF)),
-        7,
-        scalar=True,
-        scratch=(pltpu.VMEM((QROWS, C), F32), pltpu.VMEM((QROWS, C), BF), pltpu.VMEM((QROWS, C), BF)),
-    )(place, latents, blocks, input_proj, query_proj, key_proj, value_proj)
+    queries, own_queries, projected, hidden = _call(
+        query_kernel,
+        (shape((QROWS, C), BF), shape((TOK, C), BF), shape((TOK, C), F32), shape((TOK, C), BF)),
+        4,
+        scratch=(pltpu.VMEM((QROWS, C), F32), pltpu.VMEM((QROWS, C), BF)),
+    )(latents, blocks, input_proj, query_proj)
+    parts, own = _call(attend_kernel, (shape((NQ, TOK, WIDE), BF), shape((TOK, WIDE), BF)), 6)(
+        queries, own_queries, hidden, blocks, key_proj, value_proj
+    )
     parts = lax.all_to_all(parts, "patch", 0, 0, axis_index_groups=BRICKS)
-    level_out = _call(merge_kernel, shape((1, TOK, C), BF), 5)(parts, own, projected, latent, output_proj)
-    return level_out, next_hidden
+    return _call(merge_kernel, (shape((1, TOK, C), BF), shape((TOK, C), BF)), 6)(
+        parts, own, projected, hidden, latent, output_proj
+    )
 
 
 def solution(mesh):

time: 69.1 us -> 66.4 us (0.961)
  the two profiles are of different devices: /device:TPU:1 before, /device:TPU:8 now
where the time goes in v4:
time: 66.4 us; the launch traced here: 66 us
  blocking collectives  57.2 us (86%)
  Pallas kernels  7.2 us (11%)
  local copies, waits for them, and re-layouts  0.87 us (1%)
  between operations  0.7 us (1%)
    all_to_all x1, blocking collectives, on_device(): blocks = lax.all_to_all(blocks, 'patch', 0, 0, axis_index_groups=SEATS)  22.7 us
    all_to_all x1, blocking collectives, _share(): return lax.all_to_all(copies, 'patch', 0, 0, axis_index_groups=groups)  18.4 us
    all_to_all x1, blocking collectives, on_device(): parts = lax.all_to_all(parts, 'patch', 0, 0, axis_index_groups=BRICKS)  16.1 us
    pallas_call x1, Pallas kernels, on_device(): _call(attend_kernel, (shape((NQ, TOK, WIDE), BF), shape((TOK, WIDE), BF))...  2.84 us
    pallas_call x1, Pallas kernels, on_device(): _call(query_kernel, (shape((QROWS, C), BF), shape((TOK, C), BF), shape((T...  2.13 us
    pallas_call x1, Pallas kernels, on_device(): _call(merge_kernel, (shape((1, TOK, C), BF), shape((TOK, C), BF)), 6)  1.39 us

profile of v4, /device:TPU:8, one launch (start us, length us, event | category | flops | bytes accessed | tf_op | source)
XLA Modules:
  0.0 66.0 jit_solution(15729586337229374437)
XLA Ops:
  0.6 0.8 %broadcast_in_dim.8 = bf16[16,32,640]{2,1,0:T(8,128)(2,1)S(1)} broadcast(bf16[32,640]{1,0:T(8,128)(2,1)} %bitcast.1), dimensions={1,2} | broadcast | bytes 696320 | tf_op jit(solution)/shard_map/broadcast_in_dim | solution.py:223
  1.5 0.0 copy-start.6
  1.5 18.4 %all_to_all.15.latent_ref = bf16[16,32,640]{2,1,0:T(8,128)(2,1)S(1)} all-to-all(bf16[16,32,640]{2,1,0:T(8,128)(2,1)S(1)} %broadcast_in_dim.8), channel_id=1, replica_groups={{0,1,4,5,8,9,12,13,16,17,20,21,24,25,28,29},{2,3,6,7,10,11,14,15,18,19,..., dimensions={0} | all-to-all | bytes 1310720 | tf_op jit(solution)/shard_map/all_to_all | solution.py:224
  19.9 0.0 copy-done.6
  19.9 0.0 copy-start.3
  19.9 0.0 copy-start.4
  19.9 0.8 %shard_map.86 = bf16[8,176,128]{2,1,0:T(8,128)(2,1)S(1)} custom-call(bf16[16,32,640]{2,1,0:T(8,128)(2,1)S(1)} %all_to_all.15.latent_ref, bf16[32,640]{1,0:T(8,128)(2,1)S(1)} %copy-done.6), custom_call_target="tpu_custom_call" | custom-call | tf_op jit(solution)/shard_map/pallas_call | solution.py:230
  20.7 22.7 %all_to_all.16.block_ref = bf16[8,176,128]{2,1,0:T(8,128)(2,1)S(1)} all-to-all(bf16[8,176,128]{2,1,0:T(8,128)(2,1)S(1)} %shard_map.86), channel_id=1, replica_groups={{0,2,32,34,64,66,96,98},{1,3,33,35,65,67,97,99},{4,6,36,38,68,70,100,10..., dimensions={0} | all-to-all | bytes 720896 | tf_op jit(solution)/shard_map/all_to_all | solution.py:231
  43.4 0.0 copy-done.3
  43.4 0.0 copy-done.4
  43.4 0.0 copy-start.1
  43.4 0.0 copy-start.2
  43.4 2.1 %shard_map.87 = (bf16[512,640]{1,0:T(8,128)(2,1)S(1)}, bf16[32,640]{1,0:T(8,128)(2,1)S(1)}, f32[32,640]{1,0:T(8,128)S(1)}, bf16[32,640]{1,0:T(8,128)(2,1)S(1)}) custom-call(bf16[16,32,640]{2,1,0:T(8,128)(2,1)S(1)} %all_to_all.15.latent_ref, bf16[8,176,128]{2,1,0:T(8,128)(2,1)S(1)} %all_to_all.16.block_ref, bf16[640,640]{1,0:T(8,128)(2,1)S(1)} %copy-done.3, ...), custom_call_target="tpu_custom_call" | custom-call | tf_op jit(solution)/shard_map/pallas_call | solution.py:232
  45.6 0.0 copy-done.1
  45.6 0.0 copy-done.2
  45.6 2.8 %shard_map.88 = (bf16[16,32,768]{2,1,0:T(8,128)(2,1)S(1)}, bf16[32,768]{1,0:T(8,128)(2,1)S(1)}) custom-call(bf16[512,640]{1,0:T(8,128)(2,1)S(1)} %get-tuple-element.8.queries_ref, bf16[32,640]{1,0:T(8,128)(2,1)S(1)} %get-tuple-element.9.own_queries_ref, bf16[32,640]{1,0:T(8,128)(2,1)S(1)} %get-tuple-element.10.hidden_ref, ...), custom_call_target="tpu_custom_call" | custom-call | tf_op jit(solution)/shard_map/pallas_call | solution.py:238
  48.4 0.0 copy-start
  48.5 0.0 copy-start.5
  48.5 16.1 %all_to_all.17.part_ref = bf16[16,32,768]{2,1,0:T(8,128)(2,1)S(1)} all-to-all(bf16[16,32,768]{2,1,0:T(8,128)(2,1)S(1)} %get-tuple-element.11), channel_id=1, replica_groups={{0,1,4,5,8,9,12,13,16,17,20,21,24,25,28,29},{2,3,6,7,10,11,14,15,18,19,..., dimensions={0} | all-to-all | bytes 1572864 | tf_op jit(solution)/shard_map/all_to_all | solution.py:241
  64.6 0.0 copy-done
  64.6 0.0 copy-done.5
  64.6 1.4 %shard_map.89 = (bf16[1,32,640]{2,1,0:T(8,128)(2,1)}, bf16[32,640]{1,0:T(8,128)(2,1)}) custom-call(bf16[16,32,768]{2,1,0:T(8,128)(2,1)S(1)} %all_to_all.17.part_ref, bf16[32,768]{1,0:T(8,128)(2,1)S(1)} %get-tuple-element.12.own_ref, f32[32,640]{1,0:T(8,128)S(1)} %get-tuple-element.13.projected_ref, bf16[32,640]{1,0:T(8,128)(2,1)S(1)} %get-tuple-element.10.hidden_ref, ...), custom_call_target="tpu_custom_call" | custom-call | tf_op jit(solution)/shard_map/pallas_call | solution.py:242
Async XLA Ops:
  1.5 18.4 %copy-start.6 = (bf16[32,640]{1,0:T(8,128)(2,1)S(1)}, bf16[32,640]{1,0:T(8,128)(2,1)}, u32[]{:S(2)}) copy-start(bf16[32,640]{1,0:T(8,128)(2,1)} %stale_ref.1) | copy-start | bytes 122884
  19.9 23.6 %copy-start.3 = (bf16[640,640]{1,0:T(8,128)(2,1)S(1)}, bf16[640,640]{1,0:T(8,128)(2,1)}, u32[]{:S(2)}) copy-start(bf16[640,640]{1,0:T(8,128)(2,1)} %input_ref.1) | copy-start | bytes 2457604
  19.9 23.6 %copy-start.4 = (bf16[640,640]{1,0:T(8,128)(2,1)S(1)}, bf16[640,640]{1,0:T(8,128)(2,1)}, u32[]{:S(2)}) copy-start(bf16[640,640]{1,0:T(8,128)(2,1)} %query_ref.1) | copy-start | bytes 2457604
  43.4 2.1 %copy-start.1 = (bf16[640,640]{1,0:T(8,128)(2,1)S(1)}, bf16[640,640]{1,0:T(8,128)(2,1)}, u32[]{:S(2)}) copy-start(bf16[640,640]{1,0:T(8,128)(2,1)} %key_ref.1) | copy-start | bytes 2457604
  43.4 2.2 %copy-start.2 = (bf16[640,640]{1,0:T(8,128)(2,1)S(1)}, bf16[640,640]{1,0:T(8,128)(2,1)}, u32[]{:S(2)}) copy-start(bf16[640,640]{1,0:T(8,128)(2,1)} %value_ref.1) | copy-start | bytes 2457604
  48.4 16.2 %copy-start = (bf16[640,640]{1,0:T(8,128)(2,1)S(1)}, bf16[640,640]{1,0:T(8,128)(2,1)}, u32[]{:S(2)}) copy-start(bf16[640,640]{1,0:T(8,128)(2,1)} %output_ref.1) | copy-start | bytes 2457604
  48.5 16.2 %copy-start.5 = (bf16[1,32,640]{2,1,0:T(8,128)(2,1)S(1)}, bf16[1,32,640]{2,1,0:T(8,128)(2,1)}, u32[]{:S(2)}) copy-start(bf16[1,32,640]{2,1,0:T(8,128)(2,1)} %latent_ref.1) | copy-start | bytes 122884

commit v5 on v4

--- a/solution.py
+++ b/solution.py
@@ -30,8 +30,8 @@
     return [members[k] for k in sorted(members)]
 
 
-BRICKS = _groups(lambda y, x, z: (y // 2, z // 2))
-SEATS = _groups(lambda y, x, z: (y % 2, x, z % 2))
+BRICKS = _groups(lambda y, x, z: (y // 2, x // 2, z // 2))
+SEATS = _groups(lambda y, x, z: (y % 2, x % 2, z % 2))
 NQ = len(BRICKS[0])
 NK = len(SEATS[0])
 QROWS = NQ * TOK
@@ -110,12 +110,12 @@
 
 def _seat():
     me = lax.axis_index("patch")
-    return ((me >> 4) & 1) * 8 + ((me >> 2) & 3) * 2 + (me & 1)
+    return ((me >> 4) & 1) * 4 + ((me >> 2) & 1) * 2 + (me & 1)
 
 
 def _brick():
     me = lax.axis_index("patch")
-    return (me >> 5) * 2 + ((me >> 1) & 1)
+    return (me >> 5) * 4 + ((me >> 3) & 1) * 2 + ((me >> 1) & 1)
 
 
 def query_kernel(

time: 66.4 us -> 67 us (level)
  the two profiles are of different devices: /device:TPU:8 before, /device:TPU:16 now
where the time goes in v5:
time: 67 us; the launch traced here: 66.6 us
  blocking collectives  57.6 us (86%)
  Pallas kernels  7.46 us (11%)
  local copies, waits for them, and re-layouts  0.84 us (1%)
  between operations  0.71 us (1%)
    all_to_all x1, blocking collectives, on_device(): blocks = lax.all_to_all(blocks, 'patch', 0, 0, axis_index_groups=SEATS)  34.2 us
    all_to_all x1, blocking collectives, _share(): return lax.all_to_all(copies, 'patch', 0, 0, axis_index_groups=groups)  13 us
    all_to_all x1, blocking collectives, on_device(): parts = lax.all_to_all(parts, 'patch', 0, 0, axis_index_groups=BRICKS)  10.5 us
    pallas_call x1, Pallas kernels, on_device(): _call(attend_kernel, (shape((NQ, TOK, WIDE), BF), shape((TOK, WIDE), BF))...  4.22 us
    pallas_call x1, Pallas kernels, on_device(): _call(query_kernel, (shape((QROWS, C), BF), shape((TOK, C), BF), shape((T...  1.4 us

profile of v5, /device:TPU:16, one launch (start us, length us, event | category | flops | bytes accessed | tf_op | source)
XLA Modules:
  0.0 66.6 jit_solution(6004124667674237554)
XLA Ops:
  0.6 0.8 %broadcast_in_dim.8 = bf16[8,32,640]{2,1,0:T(8,128)(2,1)S(1)} broadcast(bf16[32,640]{1,0:T(8,128)(2,1)} %bitcast.1), dimensions={1,2} | broadcast | bytes 368640 | tf_op jit(solution)/shard_map/broadcast_in_dim | solution.py:223
  1.4 0.0 copy-start.6
  1.5 13.0 %all_to_all.15.latent_ref = bf16[8,32,640]{2,1,0:T(8,128)(2,1)S(1)} all-to-all(bf16[8,32,640]{2,1,0:T(8,128)(2,1)S(1)} %broadcast_in_dim.8), channel_id=1, replica_groups={{0,1,4,5,16,17,20,21},{2,3,6,7,18,19,22,23},{8,9,12,13,24,25,28,29},{10..., dimensions={0} | all-to-all | bytes 655360 | tf_op jit(solution)/shard_map/all_to_all | solution.py:224
  14.4 0.0 copy-done.6
  14.4 0.0 copy-start.4
  14.4 0.7 shard_map.86
  15.1 0.0 copy-start.3
  15.1 34.2 %all_to_all.16.block_ref = bf16[16,176,128]{2,1,0:T(8,128)(2,1)S(1)} all-to-all(bf16[16,176,128]{2,1,0:T(8,128)(2,1)S(1)} %shard_map.86), channel_id=1, replica_groups={{0,2,8,10,32,34,40,42,64,66,72,74,96,98,104,106},{1,3,9,11,33,35,41,43,..., dimensions={0} | all-to-all | bytes 1441792 | tf_op jit(solution)/shard_map/all_to_all | solution.py:231
  49.3 0.0 copy-done.4
  49.3 0.0 copy-done.3
  49.3 0.0 copy-start
  49.3 0.0 copy-start.1
  49.3 1.4 %shard_map.87 = (bf16[256,640]{1,0:T(8,128)(2,1)S(1)}, bf16[32,640]{1,0:T(8,128)(2,1)S(1)}, f32[32,640]{1,0:T(8,128)S(1)}, bf16[32,640]{1,0:T(8,128)(2,1)S(1)}) custom-call(bf16[8,32,640]{2,1,0:T(8,128)(2,1)S(1)} %all_to_all.15.latent_ref, bf16[16,176,128]{2,1,0:T(8,128)(2,1)S(1)} %all_to_all.16.block_ref, bf16[640,640]{1,0:T(8,128)(2,1)S(1)} %copy-done.3, ...), custom_call_target="tpu_custom_call" | custom-call | tf_op jit(solution)/shard_map/pallas_call | solution.py:232
  50.7 0.0 copy-done
  50.7 0.0 copy-done.1
  50.7 0.0 copy-start.2
  50.7 4.2 %shard_map.88 = (bf16[8,32,768]{2,1,0:T(8,128)(2,1)S(1)}, bf16[32,768]{1,0:T(8,128)(2,1)S(1)}) custom-call(bf16[256,640]{1,0:T(8,128)(2,1)S(1)} %get-tuple-element.8.queries_ref, bf16[32,640]{1,0:T(8,128)(2,1)S(1)} %get-tuple-element.9.own_queries_ref, bf16[32,640]{1,0:T(8,128)(2,1)S(1)} %get-tuple-element.10.hidden_ref, ...), custom_call_target="tpu_custom_call" | custom-call | tf_op jit(solution)/shard_map/pallas_call | solution.py:238
  54.9 0.0 copy-start.5
  55.0 10.5 %all_to_all.17.part_ref = bf16[8,32,768]{2,1,0:T(8,128)(2,1)S(1)} all-to-all(bf16[8,32,768]{2,1,0:T(8,128)(2,1)S(1)} %get-tuple-element.11), channel_id=1, replica_groups={{0,1,4,5,16,17,20,21},{2,3,6,7,18,19,22,23},{8,9,12,13,24,25,28,29},{10..., dimensions={0} | all-to-all | bytes 786432 | tf_op jit(solution)/shard_map/all_to_all | solution.py:241
  65.4 0.0 copy-done.2
  65.4 0.0 copy-done.5
  65.4 1.2 %shard_map.89 = (bf16[1,32,640]{2,1,0:T(8,128)(2,1)}, bf16[32,640]{1,0:T(8,128)(2,1)}) custom-call(bf16[8,32,768]{2,1,0:T(8,128)(2,1)S(1)} %all_to_all.17.part_ref, bf16[32,768]{1,0:T(8,128)(2,1)S(1)} %get-tuple-element.12.own_ref, f32[32,640]{1,0:T(8,128)S(1)} %get-tuple-element.13.projected_ref, bf16[32,640]{1,0:T(8,128)(2,1)S(1)} %get-tuple-element.10.hidden_ref, ...), custom_call_target="tpu_custom_call" | custom-call | tf_op jit(solution)/shard_map/pallas_call | solution.py:242
Async XLA Ops:
  1.4 13.0 %copy-start.6 = (bf16[32,640]{1,0:T(8,128)(2,1)S(1)}, bf16[32,640]{1,0:T(8,128)(2,1)}, u32[]{:S(2)}) copy-start(bf16[32,640]{1,0:T(8,128)(2,1)} %stale_ref.1) | copy-start | bytes 122884
  14.4 34.8 %copy-start.4 = (bf16[640,640]{1,0:T(8,128)(2,1)S(1)}, bf16[640,640]{1,0:T(8,128)(2,1)}, u32[]{:S(2)}) copy-start(bf16[640,640]{1,0:T(8,128)(2,1)} %query_ref.1) | copy-start | bytes 2457604
  15.1 34.2 %copy-start.3 = (bf16[640,640]{1,0:T(8,128)(2,1)S(1)}, bf16[640,640]{1,0:T(8,128)(2,1)}, u32[]{:S(2)}) copy-start(bf16[640,640]{1,0:T(8,128)(2,1)} %input_ref.1) | copy-start | bytes 2457604
  49.3 1.4 %copy-start = (bf16[640,640]{1,0:T(8,128)(2,1)S(1)}, bf16[640,640]{1,0:T(8,128)(2,1)}, u32[]{:S(2)}) copy-start(bf16[640,640]{1,0:T(8,128)(2,1)} %key_ref.1) | copy-start | bytes 2457604
  49.3 1.4 %copy-start.1 = (bf16[640,640]{1,0:T(8,128)(2,1)S(1)}, bf16[640,640]{1,0:T(8,128)(2,1)}, u32[]{:S(2)}) copy-start(bf16[640,640]{1,0:T(8,128)(2,1)} %value_ref.1) | copy-start | bytes 2457604
  50.7 14.7 %copy-start.2 = (bf16[640,640]{1,0:T(8,128)(2,1)S(1)}, bf16[640,640]{1,0:T(8,128)(2,1)}, u32[]{:S(2)}) copy-start(bf16[640,640]{1,0:T(8,128)(2,1)} %output_ref.1) | copy-start | bytes 2457604
  54.9 10.5 %copy-start.5 = (bf16[1,32,640]{2,1,0:T(8,128)(2,1)S(1)}, bf16[1,32,640]{2,1,0:T(8,128)(2,1)}, u32[]{:S(2)}) copy-start(bf16[1,32,640]{2,1,0:T(8,128)(2,1)} %latent_ref.1) | copy-start | bytes 122884

commit v6 on v4

--- a/solution.py
+++ b/solution.py
@@ -16,7 +16,7 @@
 LANES = 128
 SLOT = 32
 WIDE = C + LANES
-STATS = TOK * C // LANES
+STRIPS = TOK * C // LANES
 STEP = math.log2(math.e) / math.sqrt(HEAD)
 FAR = -1e30
 
@@ -64,8 +64,7 @@
     return stacked.astype(BF)
 
 
-def pack_kernel(latent_ref, stale_ref, out_ref):
-    cells = latent_ref[...].astype(F32).reshape(QROWS, C)
+def _group_stats(cells):
     to_group = _same_group((C, LANES), 0)
     to_channel = _same_group((LANES, C), 1)
 
@@ -73,15 +72,48 @@
         sums = jnp.dot(_stack_pieces(row), to_group, preferred_element_type=F32)
         return jnp.sum(sums, axis=0, keepdims=True)
 
-    center = group_sums(jnp.sum(cells, axis=0, keepdims=True)) * (1.0 / (QROWS * GROUP))
+    center = group_sums(jnp.sum(cells, axis=0, keepdims=True)) * (1.0 / (cells.shape[0] * GROUP))
     centers = jnp.dot(_stack_pieces(center), to_channel, preferred_element_type=F32)
     shifted = cells - jnp.sum(centers, axis=0, keepdims=True)
-    away = group_sums(jnp.sum(jnp.square(shifted), axis=0, keepdims=True))
-    stats = _stack_pieces(center, away)
-    for index in range(NK):
+    return center, group_sums(jnp.sum(jnp.square(shifted), axis=0, keepdims=True))
+
+
+def _join_stats(blocks_ref, count):
+    blocks = blocks_ref.shape[0]
+    stats = blocks_ref[:, STRIPS:, :].reshape(blocks * 16, LANES)
+    target = _iota((2 * blocks, blocks * 16), 0)
+    source = _iota((2 * blocks, blocks * 16), 1) - (target % blocks) * 16 - (target // blocks) * 3
+    picked = jnp.where((source >= 0) & (source < 3), 1.0, 0.0).astype(BF)
+    stats = jnp.dot(picked, stats, preferred_element_type=F32)
+    means, aways = stats[:blocks], stats[blocks:]
+    mean = jnp.sum(means, axis=0, keepdims=True) * (1.0 / blocks)
+    away = jnp.sum(aways + float(count) * jnp.square(means - mean), axis=0, keepdims=True)
+    return mean, away
+
+
+def _fill_blocks(out_ref, rows, stats):
+    for index in range(out_ref.shape[0]):
         for part in range(C // LANES):
-            out_ref[index, part * TOK : (part + 1) * TOK, :] = stale_ref[:, part * LANES : (part + 1) * LANES]
-        out_ref[index, STATS:, :] = stats
+            out_ref[index, part * TOK : (part + 1) * TOK, :] = rows[:, part * LANES : (part + 1) * LANES]
+        out_ref[index, STRIPS:, :] = stats
+
+
+def _strips(blocks_ref, first, last):
+    parts = [
+        blocks_ref[first:last, part * TOK : (part + 1) * TOK, :].reshape((last - first) * TOK, LANES)
+        for part in range(C // LANES)
+    ]
+    return jnp.concatenate(parts, axis=1)
+
+
+def far_kernel(latent_ref, stale_ref, out_ref):
+    center, away = _group_stats(latent_ref[...].reshape(TOK, C).astype(F32))
+    _fill_blocks(out_ref, stale_ref[...], _stack_pieces(center, away))
+
+
+def near_kernel(latent_ref, block_ref, out_ref):
+    mean, away = _join_stats(block_ref, TOK * GROUP)
+    _fill_blocks(out_ref, latent_ref[...].reshape(TOK, C), _stack_pieces(mean, away))
 
 
 def _attend(q_pair, k_pair, v_pair, bias):
@@ -119,43 +151,39 @@
 
 
 def query_kernel(
-    latent_ref, block_ref, input_ref, query_ref, queries_ref, own_queries_ref, projected_ref, hidden_ref, projected_all, hidden_all
+    latent_ref, input_ref, query_ref, queries_ref, own_queries_ref, projected_ref, hidden_ref, projected_all, hidden_all
 ):
     mine = pl.multiple_of(_seat() * TOK, TOK)
 
-    stats = block_ref[:, STATS:, :].reshape(NK * 16, LANES)
-    target = _iota((2 * NK, NK * 16), 0)
-    source = _iota((2 * NK, NK * 16), 1) - (target % NK) * 16 - (target // NK) * 3
-    picked = jnp.where((source >= 0) & (source < 3), 1.0, 0.0).astype(BF)
-    stats = jnp.dot(picked, stats, preferred_element_type=F32)
-    parts_mean, parts_away = stats[:NK], stats[NK:]
-    mean = jnp.sum(parts_mean, axis=0, keepdims=True) * (1.0 / NK)
-    cell_count = float(QROWS * GROUP)
-    away = jnp.sum(parts_away + cell_count * jnp.square(parts_mean - mean), axis=0, keepdims=True)
-    gain = lax.rsqrt(away * (1.0 / (cell_count * NK)) + 1e-06)
+    mean, away = _join_stats(latent_ref, KROWS * GROUP)
+    gain = lax.rsqrt(away * (1.0 / (KROWS * GROUP * NQ)) + 1e-06)
     spread = jnp.dot(_stack_pieces(mean, gain), _same_group((LANES, C), 1), preferred_element_type=F32)
     which = _iota((16, C), 0)
     center = jnp.sum(jnp.where(which < 3, spread, 0.0), axis=0, keepdims=True)
     gain = jnp.sum(jnp.where(which < 3, 0.0, spread), axis=0, keepdims=True)
-    cells = latent_ref[...].astype(F32).reshape(QROWS, C)
-    normed = ((cells - center) * gain).astype(BF)
-
-    projected = jnp.dot(normed, input_ref[...], preferred_element_type=F32)
-    projected_all[...] = projected
-    row_mean = jnp.mean(projected, axis=1, keepdims=True)
-    shifted = projected - row_mean
-    row_spread = jnp.mean(jnp.square(shifted), axis=1, keepdims=True)
-    hidden = (shifted * lax.rsqrt(row_spread + 1e-05)).astype(BF)
-    hidden_all[...] = hidden
-    queries_ref[...] = jnp.dot(hidden, query_ref[...], preferred_element_type=F32).astype(BF)
+
+    half = NQ // 2
+    projections = []
+    for index in range(2):
+        cells = _strips(latent_ref, index * half, (index + 1) * half).astype(F32)
+        normed = ((cells - center) * gain).astype(BF)
+        projections.append(jnp.dot(normed, input_ref[...], preferred_element_type=F32))
+    for index, projected in enumerate(projections):
+        rows = slice(index * half * TOK, (index + 1) * half * TOK)
+        projected_all[rows, :] = projected
+        row_mean = jnp.mean(projected, axis=1, keepdims=True)
+        shifted = projected - row_mean
+        row_spread = jnp.mean(jnp.square(shifted), axis=1, keepdims=True)
+        hidden = (shifted * lax.rsqrt(row_spread + 1e-05)).astype(BF)
+        hidden_all[rows, :] = hidden
+        queries_ref[rows, :] = jnp.dot(hidden, query_ref[...], preferred_element_type=F32).astype(BF)
     projected_ref[...] = projected_all[pl.ds(mine, TOK), :]
     hidden_ref[...] = hidden_all[pl.ds(mine, TOK), :]
     own_queries_ref[...] = queries_ref[pl.ds(mine, TOK), :]
 
 
 def attend_kernel(queries_ref, own_queries_ref, hidden_ref, block_ref, key_ref, value_ref, part_ref, own_ref):
-    strips = [block_ref[:, part * TOK : (part + 1) * TOK, :].reshape(KROWS, LANES) for part in range(C // LANES)]
-    both_hidden = jnp.concatenate([jnp.concatenate(strips, axis=1), hidden_ref[...]], axis=0)
+    both_hidden = jnp.concatenate([_strips(block_ref, 0, NK), hidden_ref[...]], axis=0)
     both_keys = jnp.dot(both_hidden, key_ref[...], preferred_element_type=F32).astype(BF)
     both_values = jnp.dot(both_hidden, value_ref[...], preferred_element_type=F32).astype(BF)
     keys, fresh_keys = both_keys[:KROWS], both_keys[KROWS:]
@@ -219,24 +247,20 @@
     )
 
 
-def _share(block, groups):
-    copies = jnp.broadcast_to(block[None], (len(groups[0]),) + block.shape)
-    return lax.all_to_all(copies, "patch", 0, 0, axis_index_groups=groups)
-
-
 def on_device(latent, stale_hidden, input_proj, query_proj, key_proj, value_proj, output_proj):
     shape = jax.ShapeDtypeStruct
-    latents = _share(latent.reshape(TOK, C), BRICKS)
-    blocks = _call(pack_kernel, shape((NK, STATS + 16, LANES), BF), 2)(latents, stale_hidden)
-    blocks = lax.all_to_all(blocks, "patch", 0, 0, axis_index_groups=SEATS)
+    stale = _call(far_kernel, shape((NK, STRIPS + 16, LANES), BF), 2)(latent, stale_hidden)
+    stale = lax.all_to_all(stale, "patch", 0, 0, axis_index_groups=SEATS)
+    latents = _call(near_kernel, shape((NQ, STRIPS + 16, LANES), BF), 2)(latent, stale)
+    latents = lax.all_to_all(latents, "patch", 0, 0, axis_index_groups=BRICKS)
     queries, own_queries, projected, hidden = _call(
         query_kernel,
         (shape((QROWS, C), BF), shape((TOK, C), BF), shape((TOK, C), F32), shape((TOK, C), BF)),
-        4,
+        3,
         scratch=(pltpu.VMEM((QROWS, C), F32), pltpu.VMEM((QROWS, C), BF)),
-    )(latents, blocks, input_proj, query_proj)
+    )(latents, input_proj, query_proj)
     parts, own = _call(attend_kernel, (shape((NQ, TOK, WIDE), BF), shape((TOK, WIDE), BF)), 6)(
-        queries, own_queries, hidden, blocks, key_proj, value_proj
+        queries, own_queries, hidden, stale, key_proj, value_proj
     )
     parts = lax.all_to_all(parts, "patch", 0, 0, axis_index_groups=BRICKS)
     return _call(merge_kernel, (shape((1, TOK, C), BF), shape((TOK, C), BF)), 6)(

time: 66.4 us -> 68.3 us (1.029)
  the two profiles are of different devices: /device:TPU:8 before, /device:TPU:16 now
where the time goes in v6:
time: 68.3 us; the launch traced here: 67.9 us
  blocking collectives  59 us (86%)
  Pallas kernels  6.61 us (10%)
  local copies, waits for them, and re-layouts  1.58 us (2%)
  between operations  0.71 us (1%)
    all_to_all x1, blocking collectives, on_device(): stale = lax.all_to_all(stale, 'patch', 0, 0, axis_index_groups=SEATS)  24.3 us
    all_to_all x1, blocking collectives, on_device(): latents = lax.all_to_all(latents, 'patch', 0, 0, axis_index_groups=BRICKS)  19 us
    all_to_all x1, blocking collectives, on_device(): parts = lax.all_to_all(parts, 'patch', 0, 0, axis_index_groups=BRICKS)  15.8 us
    pallas_call x1, Pallas kernels, on_device(): _call(attend_kernel, (shape((NQ, TOK, WIDE), BF), shape((TOK, WIDE), BF))...  2.84 us
    pallas_call x1, Pallas kernels, on_device(): _call(query_kernel, (shape((QROWS, C), BF), shape((TOK, C), BF), shape((T...  1.73 us
    unnamed x16, local copies, waits for them, and re-layouts  1.58 us
    pallas_call x1, Pallas kernels, on_device(): _call(merge_kernel, (shape((1, TOK, C), BF), shape((TOK, C), BF)), 6)  1.37 us

profile of v6, /device:TPU:16, one launch (start us, length us, event | category | flops | bytes accessed | tf_op | source)
XLA Modules:
  0.0 67.9 jit_solution(6481489141802186413)
XLA Ops:
  0.6 0.0 copy-start.5
  0.6 0.8 %copy-done.5 = bf16[1,32,640]{2,1,0:T(8,128)(2,1)S(1)} copy-done((bf16[1,32,640]{2,1,0:T(8,128)(2,1)S(1)}, bf16[1,32,640]{2,1,0:T(8,128)(2,1)}, u32[]{:S(2)}) %copy-start.5) | copy-done | bytes 40984
  1.4 0.0 copy-start.7
  1.4 0.8 %copy-done.7 = bf16[32,640]{1,0:T(8,128)(2,1)S(1)} copy-done((bf16[32,640]{1,0:T(8,128)(2,1)S(1)}, bf16[32,640]{1,0:T(8,128)(2,1)}, u32[]{:S(2)}) %copy-start.7) | copy-done | bytes 40984
  2.2 0.5 shard_map.86
  2.7 24.3 %all_to_all.15.block_ref = bf16[8,176,128]{2,1,0:T(8,128)(2,1)S(1)} all-to-all(bf16[8,176,128]{2,1,0:T(8,128)(2,1)S(1)} %shard_map.86), channel_id=1, replica_groups={{0,2,32,34,64,66,96,98},{1,3,33,35,65,67,97,99},{4,6,36,38,68,70,100,10..., dimensions={0} | all-to-all | bytes 720896 | tf_op jit(solution)/shard_map/all_to_all | solution.py:253
  27.0 0.0 copy-start.2
  27.0 0.2 shard_map.87
  27.1 0.0 copy-start.1
  27.1 19.0 %all_to_all.16.latent_ref = bf16[16,176,128]{2,1,0:T(8,128)(2,1)S(1)} all-to-all(bf16[16,176,128]{2,1,0:T(8,128)(2,1)S(1)} %shard_map.87), channel_id=1, replica_groups={{0,1,4,5,8,9,12,13,16,17,20,21,24,25,28,29},{2,3,6,7,10,11,14,15,18,19,..., dimensions={0} | all-to-all | bytes 1441792 | tf_op jit(solution)/shard_map/all_to_all | solution.py:255
  46.2 0.0 copy-done.2
  46.2 0.0 copy-done.1
  46.2 0.0 copy-start.3
  46.2 0.0 copy-start.4
  46.2 1.7 %shard_map.88 = (bf16[512,640]{1,0:T(8,128)(2,1)S(1)}, bf16[32,640]{1,0:T(8,128)(2,1)S(1)}, f32[32,640]{1,0:T(8,128)S(1)}, bf16[32,640]{1,0:T(8,128)(2,1)S(1)}) custom-call(bf16[16,176,128]{2,1,0:T(8,128)(2,1)S(1)} %all_to_all.16.latent_ref, bf16[640,640]{1,0:T(8,128)(2,1)S(1)} %copy-done.1, bf16[640,640]{1,0:T(8,128)(2,1)S(1)} %copy-done.2), custom_call_target="tpu_custom_call" | custom-call | tf_op jit(solution)/shard_map/pallas_call | solution.py:256
  47.9 0.0 copy-done.3
  47.9 0.0 copy-done.4
  47.9 2.8 %shard_map.89 = (bf16[16,32,768]{2,1,0:T(8,128)(2,1)S(1)}, bf16[32,768]{1,0:T(8,128)(2,1)S(1)}) custom-call(bf16[512,640]{1,0:T(8,128)(2,1)S(1)} %get-tuple-element.8.queries_ref, bf16[32,640]{1,0:T(8,128)(2,1)S(1)} %get-tuple-element.9.own_queries_ref, bf16[32,640]{1,0:T(8,128)(2,1)S(1)} %get-tuple-element.10.hidden_ref, ...), custom_call_target="tpu_custom_call" | custom-call | tf_op jit(solution)/shard_map/pallas_call | solution.py:262
  50.8 0.0 copy-start
  50.8 0.0 copy-start.6
  50.8 15.8 %all_to_all.17.part_ref = bf16[16,32,768]{2,1,0:T(8,128)(2,1)S(1)} all-to-all(bf16[16,32,768]{2,1,0:T(8,128)(2,1)S(1)} %get-tuple-element.11), channel_id=1, replica_groups={{0,1,4,5,8,9,12,13,16,17,20,21,24,25,28,29},{2,3,6,7,10,11,14,15,18,19,..., dimensions={0} | all-to-all | bytes 1572864 | tf_op jit(solution)/shard_map/all_to_all | solution.py:265
  66.6 0.0 copy-done
  66.6 0.0 copy-done.6
  66.6 1.4 %shard_map.90 = (bf16[1,32,640]{2,1,0:T(8,128)(2,1)}, bf16[32,640]{1,0:T(8,128)(2,1)}) custom-call(bf16[16,32,768]{2,1,0:T(8,128)(2,1)S(1)} %all_to_all.17.part_ref, bf16[32,768]{1,0:T(8,128)(2,1)S(1)} %get-tuple-element.12.own_ref, f32[32,640]{1,0:T(8,128)S(1)} %get-tuple-element.13.projected_ref, bf16[32,640]{1,0:T(8,128)(2,1)S(1)} %get-tuple-element.10.hidden_ref, ...), custom_call_target="tpu_custom_call" | custom-call | tf_op jit(solution)/shard_map/pallas_call | solution.py:266
Async XLA Ops:
  0.6 0.8 %copy-start.5 = (bf16[1,32,640]{2,1,0:T(8,128)(2,1)S(1)}, bf16[1,32,640]{2,1,0:T(8,128)(2,1)}, u32[]{:S(2)}) copy-start(bf16[1,32,640]{2,1,0:T(8,128)(2,1)} %latent_ref.5) | copy-start | bytes 122884
  1.4 0.8 %copy-start.7 = (bf16[32,640]{1,0:T(8,128)(2,1)S(1)}, bf16[32,640]{1,0:T(8,128)(2,1)}, u32[]{:S(2)}) copy-start(bf16[32,640]{1,0:T(8,128)(2,1)} %stale_ref.1) | copy-start | bytes 122884
  27.0 19.2 %copy-start.2 = (bf16[640,640]{1,0:T(8,128)(2,1)S(1)}, bf16[640,640]{1,0:T(8,128)(2,1)}, u32[]{:S(2)}) copy-start(bf16[640,640]{1,0:T(8,128)(2,1)} %query_ref.1) | copy-start | bytes 2457604
  27.1 19.0 %copy-start.1 = (bf16[640,640]{1,0:T(8,128)(2,1)S(1)}, bf16[640,640]{1,0:T(8,128)(2,1)}, u32[]{:S(2)}) copy-start(bf16[640,640]{1,0:T(8,128)(2,1)} %input_ref.1) | copy-start | bytes 2457604
  46.2 1.7 %copy-start.3 = (bf16[640,640]{1,0:T(8,128)(2,1)S(1)}, bf16[640,640]{1,0:T(8,128)(2,1)}, u32[]{:S(2)}) copy-start(bf16[640,640]{1,0:T(8,128)(2,1)} %key_ref.1) | copy-start | bytes 2457604
  46.2 1.8 %copy-start.4 = (bf16[640,640]{1,0:T(8,128)(2,1)S(1)}, bf16[640,640]{1,0:T(8,128)(2,1)}, u32[]{:S(2)}) copy-start(bf16[640,640]{1,0:T(8,128)(2,1)} %value_ref.1) | copy-start | bytes 2457604
  50.8 15.8 %copy-start = (bf16[640,640]{1,0:T(8,128)(2,1)S(1)}, bf16[640,640]{1,0:T(8,128)(2,1)}, u32[]{:S(2)}) copy-start(bf16[640,640]{1,0:T(8,128)(2,1)} %output_ref.1) | copy-start | bytes 2457604
  50.8 15.8 %copy-start.6 = (bf16[1,32,640]{2,1,0:T(8,128)(2,1)S(1)}, bf16[1,32,640]{2,1,0:T(8,128)(2,1)}, u32[]{:S(2)}) copy-start(bf16[1,32,640]{2,1,0:T(8,128)(2,1)} %latent_ref.5) | copy-start | bytes 122884

commit v7 on v6

--- a/solution.py
+++ b/solution.py
@@ -106,9 +106,17 @@
     return jnp.concatenate(parts, axis=1)
 
 
-def far_kernel(latent_ref, stale_ref, out_ref):
-    center, away = _group_stats(latent_ref[...].reshape(TOK, C).astype(F32))
-    _fill_blocks(out_ref, stale_ref[...], _stack_pieces(center, away))
+def far_kernel(latent_ref, stale_ref, out_ref, latent, stale, arrived):
+    pulls = (
+        pltpu.make_async_copy(latent_ref, latent, arrived.at[0]),
+        pltpu.make_async_copy(stale_ref, stale, arrived.at[1]),
+    )
+    for pull in pulls:
+        pull.start()
+    for pull in pulls:
+        pull.wait()
+    center, away = _group_stats(latent[...].reshape(TOK, C).astype(F32))
+    _fill_blocks(out_ref, stale[...], _stack_pieces(center, away))
 
 
 def near_kernel(latent_ref, block_ref, out_ref):
@@ -233,8 +241,8 @@
     level_ref[...] = level.astype(BF).reshape(1, TOK, C)
 
 
-def _call(kernel, out_shape, n_in, scratch=(), limit=16 * 2**20):
-    specs = [pl.BlockSpec(memory_space=pltpu.VMEM)] * n_in
+def _call(kernel, out_shape, n_in, place=pltpu.VMEM, scratch=(), limit=16 * 2**20):
+    specs = [pl.BlockSpec(memory_space=place)] * n_in
     several = isinstance(out_shape, tuple)
     whole = pl.BlockSpec(memory_space=pltpu.VMEM)
     return pl.pallas_call(
@@ -249,7 +257,13 @@
 
 def on_device(latent, stale_hidden, input_proj, query_proj, key_proj, value_proj, output_proj):
     shape = jax.ShapeDtypeStruct
-    stale = _call(far_kernel, shape((NK, STRIPS + 16, LANES), BF), 2)(latent, stale_hidden)
+    stale = _call(
+        far_kernel,
+        shape((NK, STRIPS + 16, LANES), BF),
+        2,
+        place=pltpu.HBM,
+        scratch=(pltpu.VMEM(latent.shape, BF), pltpu.VMEM(stale_hidden.shape, BF), pltpu.SemaphoreType.DMA((2,))),
+    )(latent, stale_hidden)
     stale = lax.all_to_all(stale, "patch", 0, 0, axis_index_groups=SEATS)
     latents = _call(near_kernel, shape((NQ, STRIPS + 16, LANES), BF), 2)(latent, stale)
     latents = lax.all_to_all(latents, "patch", 0, 0, axis_index_groups=BRICKS)

time: 68.3 us -> 68.4 us (level)
  no operation moved by 1% of the time
where the time goes in v7:
time: 68.4 us; the launch traced here: 68.1 us
  blocking collectives  59 us (86%)
  Pallas kernels  6.73 us (10%)
  local copies, waits for them, and re-layouts  1.58 us (2%)
  between operations  0.71 us (1%)
    all_to_all x1, blocking collectives, on_device(): stale = lax.all_to_all(stale, 'patch', 0, 0, axis_index_groups=SEATS)  24.3 us
    all_to_all x1, blocking collectives, on_device(): latents = lax.all_to_all(latents, 'patch', 0, 0, axis_index_groups=BRICKS)  19 us
    all_to_all x1, blocking collectives, on_device(): parts = lax.all_to_all(parts, 'patch', 0, 0, axis_index_groups=BRICKS)  15.8 us
    pallas_call x1, Pallas kernels, on_device(): _call(attend_kernel, (shape((NQ, TOK, WIDE), BF), shape((TOK, WIDE), BF))...  2.84 us
    pallas_call x1, Pallas kernels, on_device(): _call(query_kernel, (shape((QROWS, C), BF), shape((TOK, C), BF), shape((T...  1.73 us
    unnamed x16, local copies, waits for them, and re-layouts  1.58 us
    pallas_call x1, Pallas kernels, on_device(): _call(merge_kernel, (shape((1, TOK, C), BF), shape((TOK, C), BF)), 6)  1.37 us

profile of v7, /device:TPU:16, one launch (start us, length us, event | category | flops | bytes accessed | tf_op | source)
XLA Modules:
  0.0 68.1 jit_solution(16625043435348034652)
XLA Ops:
  0.6 0.0 copy-start.5
  0.6 0.8 %copy-done.5 = bf16[1,32,640]{2,1,0:T(8,128)(2,1)S(1)} copy-done((bf16[1,32,640]{2,1,0:T(8,128)(2,1)S(1)}, bf16[1,32,640]{2,1,0:T(8,128)(2,1)}, u32[]{:S(2)}) %copy-start.5) | copy-done | bytes 40984
  1.4 0.0 copy-start.7
  1.4 0.8 %copy-done.7 = bf16[32,640]{1,0:T(8,128)(2,1)S(1)} copy-done((bf16[32,640]{1,0:T(8,128)(2,1)S(1)}, bf16[32,640]{1,0:T(8,128)(2,1)}, u32[]{:S(2)}) %copy-start.7) | copy-done | bytes 40984
  2.2 0.6 shard_map.86
  2.8 24.3 %all_to_all.15.block_ref = bf16[8,176,128]{2,1,0:T(8,128)(2,1)S(1)} all-to-all(bf16[8,176,128]{2,1,0:T(8,128)(2,1)S(1)} %shard_map.86), channel_id=1, replica_groups={{0,2,32,34,64,66,96,98},{1,3,33,35,65,67,97,99},{4,6,36,38,68,70,100,10..., dimensions={0} | all-to-all | bytes 720896 | tf_op jit(solution)/shard_map/all_to_all | solution.py:267
  27.1 0.0 copy-start.2
  27.1 0.2 shard_map.87
  27.3 0.0 copy-start.1
  27.3 19.0 %all_to_all.16.latent_ref = bf16[16,176,128]{2,1,0:T(8,128)(2,1)S(1)} all-to-all(bf16[16,176,128]{2,1,0:T(8,128)(2,1)S(1)} %shard_map.87), channel_id=1, replica_groups={{0,1,4,5,8,9,12,13,16,17,20,21,24,25,28,29},{2,3,6,7,10,11,14,15,18,19,..., dimensions={0} | all-to-all | bytes 1441792 | tf_op jit(solution)/shard_map/all_to_all | solution.py:269
  46.3 0.0 copy-done.2
  46.3 0.0 copy-done.1
  46.3 0.0 copy-start.3
  46.3 0.0 copy-start.4
  46.3 1.7 %shard_map.88 = (bf16[512,640]{1,0:T(8,128)(2,1)S(1)}, bf16[32,640]{1,0:T(8,128)(2,1)S(1)}, f32[32,640]{1,0:T(8,128)S(1)}, bf16[32,640]{1,0:T(8,128)(2,1)S(1)}) custom-call(bf16[16,176,128]{2,1,0:T(8,128)(2,1)S(1)} %all_to_all.16.latent_ref, bf16[640,640]{1,0:T(8,128)(2,1)S(1)} %copy-done.1, bf16[640,640]{1,0:T(8,128)(2,1)S(1)} %copy-done.2), custom_call_target="tpu_custom_call" | custom-call | tf_op jit(solution)/shard_map/pallas_call | solution.py:270
  48.0 0.0 copy-done.3
  48.0 0.0 copy-done.4
  48.0 2.8 %shard_map.89 = (bf16[16,32,768]{2,1,0:T(8,128)(2,1)S(1)}, bf16[32,768]{1,0:T(8,128)(2,1)S(1)}) custom-call(bf16[512,640]{1,0:T(8,128)(2,1)S(1)} %get-tuple-element.8.queries_ref, bf16[32,640]{1,0:T(8,128)(2,1)S(1)} %get-tuple-element.9.own_queries_ref, bf16[32,640]{1,0:T(8,128)(2,1)S(1)} %get-tuple-element.10.hidden_ref, ...), custom_call_target="tpu_custom_call" | custom-call | tf_op jit(solution)/shard_map/pallas_call | solution.py:276
  50.9 0.0 copy-start
  50.9 0.0 copy-start.6
  50.9 15.8 %all_to_all.17.part_ref = bf16[16,32,768]{2,1,0:T(8,128)(2,1)S(1)} all-to-all(bf16[16,32,768]{2,1,0:T(8,128)(2,1)S(1)} %get-tuple-element.11), channel_id=1, replica_groups={{0,1,4,5,8,9,12,13,16,17,20,21,24,25,28,29},{2,3,6,7,10,11,14,15,18,19,..., dimensions={0} | all-to-all | bytes 1572864 | tf_op jit(solution)/shard_map/all_to_all | solution.py:279
  66.7 0.0 copy-done
  66.7 0.0 copy-done.6
  66.7 1.4 %shard_map.90 = (bf16[1,32,640]{2,1,0:T(8,128)(2,1)}, bf16[32,640]{1,0:T(8,128)(2,1)}) custom-call(bf16[16,32,768]{2,1,0:T(8,128)(2,1)S(1)} %all_to_all.17.part_ref, bf16[32,768]{1,0:T(8,128)(2,1)S(1)} %get-tuple-element.12.own_ref, f32[32,640]{1,0:T(8,128)S(1)} %get-tuple-element.13.projected_ref, bf16[32,640]{1,0:T(8,128)(2,1)S(1)} %get-tuple-element.10.hidden_ref, ...), custom_call_target="tpu_custom_call" | custom-call | tf_op jit(solution)/shard_map/pallas_call | solution.py:280
Async XLA Ops:
  0.6 0.8 %copy-start.5 = (bf16[1,32,640]{2,1,0:T(8,128)(2,1)S(1)}, bf16[1,32,640]{2,1,0:T(8,128)(2,1)}, u32[]{:S(2)}) copy-start(bf16[1,32,640]{2,1,0:T(8,128)(2,1)} %latent_ref.5) | copy-start | bytes 122884
  1.4 0.8 %copy-start.7 = (bf16[32,640]{1,0:T(8,128)(2,1)S(1)}, bf16[32,640]{1,0:T(8,128)(2,1)}, u32[]{:S(2)}) copy-start(bf16[32,640]{1,0:T(8,128)(2,1)} %stale_ref.1) | copy-start | bytes 122884
  27.1 19.2 %copy-start.2 = (bf16[640,640]{1,0:T(8,128)(2,1)S(1)}, bf16[640,640]{1,0:T(8,128)(2,1)}, u32[]{:S(2)}) copy-start(bf16[640,640]{1,0:T(8,128)(2,1)} %query_ref.1) | copy-start | bytes 2457604
  27.3 19.0 %copy-start.1 = (bf16[640,640]{1,0:T(8,128)(2,1)S(1)}, bf16[640,640]{1,0:T(8,128)(2,1)}, u32[]{:S(2)}) copy-start(bf16[640,640]{1,0:T(8,128)(2,1)} %input_ref.1) | copy-start | bytes 2457604
  46.3 1.7 %copy-start.3 = (bf16[640,640]{1,0:T(8,128)(2,1)S(1)}, bf16[640,640]{1,0:T(8,128)(2,1)}, u32[]{:S(2)}) copy-start(bf16[640,640]{1,0:T(8,128)(2,1)} %key_ref.1) | copy-start | bytes 2457604
  46.3 1.8 %copy-start.4 = (bf16[640,640]{1,0:T(8,128)(2,1)S(1)}, bf16[640,640]{1,0:T(8,128)(2,1)}, u32[]{:S(2)}) copy-start(bf16[640,640]{1,0:T(8,128)(2,1)} %value_ref.1) | copy-start | bytes 2457604
  50.9 15.8 %copy-start = (bf16[640,640]{1,0:T(8,128)(2,1)S(1)}, bf16[640,640]{1,0:T(8,128)(2,1)}, u32[]{:S(2)}) copy-start(bf16[640,640]{1,0:T(8,128)(2,1)} %output_ref.1) | copy-start | bytes 2457604
  50.9 15.8 %copy-start.6 = (bf16[1,32,640]{2,1,0:T(8,128)(2,1)S(1)}, bf16[1,32,640]{2,1,0:T(8,128)(2,1)}, u32[]{:S(2)}) copy-start(bf16[1,32,640]{2,1,0:T(8,128)(2,1)} %latent_ref.5) | copy-start | bytes 122884

commit v8 on v5

--- a/solution.py
+++ b/solution.py
@@ -30,8 +30,8 @@
     return [members[k] for k in sorted(members)]
 
 
-BRICKS = _groups(lambda y, x, z: (y // 2, x // 2, z // 2))
-SEATS = _groups(lambda y, x, z: (y % 2, x % 2, z % 2))
+BRICKS = _groups(lambda y, x, z: (y, z // 2))
+SEATS = _groups(lambda y, x, z: (x, z % 2))
 NQ = len(BRICKS[0])
 NK = len(SEATS[0])
 QROWS = NQ * TOK
@@ -82,6 +82,30 @@
         for part in range(C // LANES):
             out_ref[index, part * TOK : (part + 1) * TOK, :] = stale_ref[:, part * LANES : (part + 1) * LANES]
         out_ref[index, STATS:, :] = stats
+
+
+def _attend_own(queries, keys, values, out_ref):
+    head = _iota((TOK, C), 1) // HEAD
+    zero = jnp.zeros_like(queries)
+    stacked = jnp.concatenate([jnp.where(head == h, queries, zero) for h in range(HEADS)], axis=0)
+    scores = lax.dot_general(stacked, keys, (((1,), (1,)), ((), ())), preferred_element_type=F32)
+    top = jnp.max(scores, axis=1, keepdims=True)
+    weights = jnp.exp2((scores - top) * STEP).astype(BF)
+    ones = jnp.ones((TOK, LANES), BF)
+    sums = jnp.dot(weights, jnp.concatenate([values, ones], axis=1), preferred_element_type=F32)
+    total = sums[:, C:]
+    scale = 1.0 / total
+    logs = top * STEP + jnp.log2(total)
+    left = _iota((TOK, LANES), 1) < HEAD
+    lane = _iota((TOK, LANES), 1) % SLOT
+    packed = jnp.zeros((TOK, LANES), F32)
+    for pair in range(HEADS // 2):
+        cut = slice(pair * LANES, (pair + 1) * LANES)
+        low = slice(2 * pair * TOK, (2 * pair + 1) * TOK)
+        high = slice((2 * pair + 1) * TOK, (2 * pair + 2) * TOK)
+        out_ref[:, cut] = jnp.where(left, sums[low, cut] * scale[low], sums[high, cut] * scale[high]).astype(BF)
+        packed = jnp.where(lane == 2 * pair, logs[low], jnp.where(lane == 2 * pair + 1, logs[high], packed))
+    out_ref[:, C:] = _pack_logs(packed)
 
 
 def _attend(q_pair, k_pair, v_pair, bias):
@@ -110,12 +134,12 @@
 
 def _seat():
     me = lax.axis_index("patch")
-    return ((me >> 4) & 1) * 4 + ((me >> 2) & 1) * 2 + (me & 1)
+    return ((me >> 2) & 3) * 2 + (me & 1)
 
 
 def _brick():
     me = lax.axis_index("patch")
-    return (me >> 5) * 4 + ((me >> 3) & 1) * 2 + ((me >> 1) & 1)
+    return (me >> 4) * 2 + ((me >> 1) & 1)
 
 
 def query_kernel(
@@ -137,17 +161,22 @@
     which = _iota((16, C), 0)
     center = jnp.sum(jnp.where(which < 3, spread, 0.0), axis=0, keepdims=True)
     gain = jnp.sum(jnp.where(which < 3, 0.0, spread), axis=0, keepdims=True)
-    cells = latent_ref[...].astype(F32).reshape(QROWS, C)
-    normed = ((cells - center) * gain).astype(BF)
-
-    projected = jnp.dot(normed, input_ref[...], preferred_element_type=F32)
-    projected_all[...] = projected
-    row_mean = jnp.mean(projected, axis=1, keepdims=True)
-    shifted = projected - row_mean
-    row_spread = jnp.mean(jnp.square(shifted), axis=1, keepdims=True)
-    hidden = (shifted * lax.rsqrt(row_spread + 1e-05)).astype(BF)
-    hidden_all[...] = hidden
-    queries_ref[...] = jnp.dot(hidden, query_ref[...], preferred_element_type=F32).astype(BF)
+    step = QROWS // 2
+    starts = range(0, QROWS, step)
+    projections = []
+    for start in starts:
+        cells = latent_ref[start // TOK : (start + step) // TOK].astype(F32).reshape(step, C)
+        normed = ((cells - center) * gain).astype(BF)
+        projections.append(jnp.dot(normed, input_ref[...], preferred_element_type=F32))
+    for start, projected in zip(starts, projections):
+        rows = slice(start, start + step)
+        projected_all[rows, :] = projected
+        row_mean = jnp.mean(projected, axis=1, keepdims=True)
+        shifted = projected - row_mean
+        row_spread = jnp.mean(jnp.square(shifted), axis=1, keepdims=True)
+        hidden = (shifted * lax.rsqrt(row_spread + 1e-05)).astype(BF)
+        hidden_all[rows, :] = hidden
+        queries_ref[rows, :] = jnp.dot(hidden, query_ref[...], preferred_element_type=F32).astype(BF)
     projected_ref[...] = projected_all[pl.ds(mine, TOK), :]
     hidden_ref[...] = hidden_all[pl.ds(mine, TOK), :]
     own_queries_ref[...] = queries_ref[pl.ds(mine, TOK), :]
@@ -166,21 +195,14 @@
     bias = jnp.where((row_band == _seat()) & (col_band == _brick()), FAR, 0.0).astype(F32)
 
     lane = _iota((QROWS, LANES), 1) % SLOT
-    own_lane = _iota((TOK, LANES), 1) % SLOT
     logs = jnp.zeros((QROWS, LANES), F32)
-    own_logs = jnp.zeros((TOK, LANES), F32)
     for pair in range(HEADS // 2):
         cut = slice(pair * LANES, (pair + 1) * LANES)
         mixed, low, high = _attend(queries_ref[:, cut], keys[:, cut], values[:, cut], bias)
         part_ref[:, :, cut] = mixed.astype(BF).reshape(NQ, TOK, LANES)
         logs = jnp.where(lane == 2 * pair, low, jnp.where(lane == 2 * pair + 1, high, logs))
-        mixed, low, high = _attend(
-            own_queries_ref[:, cut], fresh_keys[:, cut], fresh_values[:, cut], None
-        )
-        own_ref[:, cut] = mixed.astype(BF)
-        own_logs = jnp.where(own_lane == 2 * pair, low, jnp.where(own_lane == 2 * pair + 1, high, own_logs))
     part_ref[:, :, C:] = _pack_logs(logs).reshape(NQ, TOK, LANES)
-    own_ref[:, C:] = _pack_logs(own_logs)
+    _attend_own(own_queries_ref[...], fresh_keys, fresh_values, own_ref)
 
 
 def merge_kernel(part_ref, own_ref, projected_ref, hidden_ref, latent_ref, output_ref, level_ref, next_ref):

time: 67 us -> 64.9 us (0.969)
  the two profiles are of different devices: /device:TPU:16 before, /device:TPU:8 now
where the time goes in v8:
time: 64.9 us; the launch traced here: 64.5 us
  blocking collectives  56.1 us (86%)
  Pallas kernels  6.71 us (10%)
  local copies, waits for them, and re-layouts  0.96 us (1%)
  between operations  0.69 us (1%)
    all_to_all x1, blocking collectives, on_device(): blocks = lax.all_to_all(blocks, 'patch', 0, 0, axis_index_groups=SEATS)  31.3 us
    all_to_all x1, blocking collectives, _share(): return lax.all_to_all(copies, 'patch', 0, 0, axis_index_groups=groups)  14 us
    all_to_all x1, blocking collectives, on_device(): parts = lax.all_to_all(parts, 'patch', 0, 0, axis_index_groups=BRICKS)  10.8 us
    pallas_call x1, Pallas kernels, on_device(): _call(attend_kernel, (shape((NQ, TOK, WIDE), BF), shape((TOK, WIDE), BF))...  3.63 us

profile of v8, /device:TPU:8, one launch (start us, length us, event | category | flops | bytes accessed | tf_op | source)
XLA Modules:
  0.0 64.5 jit_solution(8831509752438734536)
XLA Ops:
  0.6 0.8 %broadcast_in_dim.8 = bf16[8,32,640]{2,1,0:T(8,128)(2,1)S(1)} broadcast(bf16[32,640]{1,0:T(8,128)(2,1)} %bitcast.1), dimensions={1,2} | broadcast | bytes 368640 | tf_op jit(solution)/shard_map/broadcast_in_dim | solution.py:245
  1.4 0.0 copy-start.6
  1.5 14.0 %all_to_all.15.latent_ref = bf16[8,32,640]{2,1,0:T(8,128)(2,1)S(1)} all-to-all(bf16[8,32,640]{2,1,0:T(8,128)(2,1)S(1)} %broadcast_in_dim.8), channel_id=1, replica_groups={{0,1,4,5,8,9,12,13},{2,3,6,7,10,11,14,15},{16,17,20,21,24,25,28,29},{18..., dimensions={0} | all-to-all | bytes 655360 | tf_op jit(solution)/shard_map/all_to_all | solution.py:246
  15.4 0.0 copy-done.6
  15.5 0.0 copy-start.4
  15.5 0.7 %shard_map.86 = bf16[16,176,128]{2,1,0:T(8,128)(2,1)S(1)} custom-call(bf16[8,32,640]{2,1,0:T(8,128)(2,1)S(1)} %all_to_all.15.latent_ref, bf16[32,640]{1,0:T(8,128)(2,1)S(1)} %copy-done.6), custom_call_target="tpu_custom_call" | custom-call | tf_op jit(solution)/shard_map/pallas_call | solution.py:252
  16.1 0.0 copy-start.3
  16.1 31.3 %all_to_all.16.block_ref = bf16[16,176,128]{2,1,0:T(8,128)(2,1)S(1)} all-to-all(bf16[16,176,128]{2,1,0:T(8,128)(2,1)S(1)} %shard_map.86), channel_id=1, replica_groups={{0,2,16,18,32,34,48,50,64,66,80,82,96,98,112,114},{1,3,17,19,33,35,49,5..., dimensions={0} | all-to-all | bytes 1441792 | tf_op jit(solution)/shard_map/all_to_all | solution.py:253
  47.4 0.0 copy-done.4
  47.4 0.0 copy-done.3
  47.4 0.0 copy-start
  47.5 0.0 copy-start.1
  47.5 1.2 %shard_map.87 = (bf16[256,640]{1,0:T(8,128)(2,1)S(1)}, bf16[32,640]{1,0:T(8,128)(2,1)S(1)}, f32[32,640]{1,0:T(8,128)S(1)}, bf16[32,640]{1,0:T(8,128)(2,1)S(1)}) custom-call(bf16[8,32,640]{2,1,0:T(8,128)(2,1)S(1)} %all_to_all.15.latent_ref, bf16[16,176,128]{2,1,0:T(8,128)(2,1)S(1)} %all_to_all.16.block_ref, bf16[640,640]{1,0:T(8,128)(2,1)S(1)} %copy-done.3, ...), custom_call_target="tpu_custom_call" | custom-call | tf_op jit(solution)/shard_map/pallas_call | solution.py:254
  48.7 0.0 copy-done
  48.7 0.1 copy-done.1
  48.8 0.0 copy-start.2
  48.8 3.6 %shard_map.88 = (bf16[8,32,768]{2,1,0:T(8,128)(2,1)S(1)}, bf16[32,768]{1,0:T(8,128)(2,1)S(1)}) custom-call(bf16[256,640]{1,0:T(8,128)(2,1)S(1)} %get-tuple-element.8.queries_ref, bf16[32,640]{1,0:T(8,128)(2,1)S(1)} %get-tuple-element.9.own_queries_ref, bf16[32,640]{1,0:T(8,128)(2,1)S(1)} %get-tuple-element.10.hidden_ref, ...), custom_call_target="tpu_custom_call" | custom-call | tf_op jit(solution)/shard_map/pallas_call | solution.py:260
  52.5 0.0 copy-start.5
  52.5 10.8 %all_to_all.17.part_ref = bf16[8,32,768]{2,1,0:T(8,128)(2,1)S(1)} all-to-all(bf16[8,32,768]{2,1,0:T(8,128)(2,1)S(1)} %get-tuple-element.11), channel_id=1, replica_groups={{0,1,4,5,8,9,12,13},{2,3,6,7,10,11,14,15},{16,17,20,21,24,25,28,29},{18..., dimensions={0} | all-to-all | bytes 786432 | tf_op jit(solution)/shard_map/all_to_all | solution.py:263
  63.3 0.0 copy-done.2
  63.3 0.0 copy-done.5
  63.3 1.2 %shard_map.89 = (bf16[1,32,640]{2,1,0:T(8,128)(2,1)}, bf16[32,640]{1,0:T(8,128)(2,1)}) custom-call(bf16[8,32,768]{2,1,0:T(8,128)(2,1)S(1)} %all_to_all.17.part_ref, bf16[32,768]{1,0:T(8,128)(2,1)S(1)} %get-tuple-element.12.own_ref, f32[32,640]{1,0:T(8,128)S(1)} %get-tuple-element.13.projected_ref, bf16[32,640]{1,0:T(8,128)(2,1)S(1)} %get-tuple-element.10.hidden_ref, ...), custom_call_target="tpu_custom_call" | custom-call | tf_op jit(solution)/shard_map/pallas_call | solution.py:264
Async XLA Ops:
  1.4 14.0 %copy-start.6 = (bf16[32,640]{1,0:T(8,128)(2,1)S(1)}, bf16[32,640]{1,0:T(8,128)(2,1)}, u32[]{:S(2)}) copy-start(bf16[32,640]{1,0:T(8,128)(2,1)} %stale_ref.1) | copy-start | bytes 122884
  15.5 32.0 %copy-start.4 = (bf16[640,640]{1,0:T(8,128)(2,1)S(1)}, bf16[640,640]{1,0:T(8,128)(2,1)}, u32[]{:S(2)}) copy-start(bf16[640,640]{1,0:T(8,128)(2,1)} %query_ref.1) | copy-start | bytes 2457604
  16.1 31.3 %copy-start.3 = (bf16[640,640]{1,0:T(8,128)(2,1)S(1)}, bf16[640,640]{1,0:T(8,128)(2,1)}, u32[]{:S(2)}) copy-start(bf16[640,640]{1,0:T(8,128)(2,1)} %input_ref.1) | copy-start | bytes 2457604
  47.4 1.3 %copy-start = (bf16[640,640]{1,0:T(8,128)(2,1)S(1)}, bf16[640,640]{1,0:T(8,128)(2,1)}, u32[]{:S(2)}) copy-start(bf16[640,640]{1,0:T(8,128)(2,1)} %key_ref.1) | copy-start | bytes 2457604
  47.5 1.4 %copy-start.1 = (bf16[640,640]{1,0:T(8,128)(2,1)S(1)}, bf16[640,640]{1,0:T(8,128)(2,1)}, u32[]{:S(2)}) copy-start(bf16[640,640]{1,0:T(8,128)(2,1)} %value_ref.1) | copy-start | bytes 2457604
  48.8 14.4 %copy-start.2 = (bf16[640,640]{1,0:T(8,128)(2,1)S(1)}, bf16[640,640]{1,0:T(8,128)(2,1)}, u32[]{:S(2)}) copy-start(bf16[640,640]{1,0:T(8,128)(2,1)} %output_ref.1) | copy-start | bytes 2457604
  52.5 10.8 %copy-start.5 = (bf16[1,32,640]{2,1,0:T(8,128)(2,1)S(1)}, bf16[1,32,640]{2,1,0:T(8,128)(2,1)}, u32[]{:S(2)}) copy-start(bf16[1,32,640]{2,1,0:T(8,128)(2,1)} %latent_ref.1) | copy-start | bytes 122884

commit v9 on v8

--- a/solution.py
+++ b/solution.py
@@ -17,6 +17,7 @@
 SLOT = 32
 WIDE = C + LANES
 STATS = TOK * C // LANES
+STAT_ROWS = 8
 STEP = math.log2(math.e) / math.sqrt(HEAD)
 FAR = -1e30
 
@@ -56,9 +57,9 @@
     return jnp.where((_iota(shape, channel_axis) * 52429) >> 20 == _iota(shape, group_axis), 1.0, 0.0).astype(BF)
 
 
-def _stack_pieces(*rows):
-    which = _iota((16, rows[0].shape[1]), 0)
-    stacked = jnp.zeros((16, rows[0].shape[1]), F32)
+def _stack_pieces(*rows, height=16):
+    which = _iota((height, rows[0].shape[1]), 0)
+    stacked = jnp.zeros((height, rows[0].shape[1]), F32)
     for index, piece in enumerate(p for row in rows for p in _pieces(row)):
         stacked = jnp.where(which == index, piece, stacked)
     return stacked.astype(BF)
@@ -77,7 +78,7 @@
     centers = jnp.dot(_stack_pieces(center), to_channel, preferred_element_type=F32)
     shifted = cells - jnp.sum(centers, axis=0, keepdims=True)
     away = group_sums(jnp.sum(jnp.square(shifted), axis=0, keepdims=True))
-    stats = _stack_pieces(center, away)
+    stats = _stack_pieces(center, away, height=STAT_ROWS)
     for index in range(NK):
         for part in range(C // LANES):
             out_ref[index, part * TOK : (part + 1) * TOK, :] = stale_ref[:, part * LANES : (part + 1) * LANES]
@@ -111,9 +112,14 @@
 def _attend(q_pair, k_pair, v_pair, bias):
     rows = q_pair.shape[0]
     left = _iota((rows, LANES), 1) < HEAD
-    zero = jnp.zeros_like(q_pair)
-    both = jnp.concatenate([jnp.where(left, q_pair, zero), jnp.where(left, zero, q_pair)], axis=0)
-    scores = lax.dot_general(both, k_pair, (((1,), (1,)), ((), ())), preferred_element_type=F32)
+    dims = (((1,), (1,)), ((), ()))
+    scores = jnp.concatenate(
+        [
+            lax.dot_general(q_pair[:, cut], k_pair[:, cut], dims, preferred_element_type=F32)
+            for cut in (slice(0, HEAD), slice(HEAD, 2 * HEAD))
+        ],
+        axis=0,
+    )
     if bias is not None:
         scores = scores + bias
     top = jnp.max(scores, axis=1, keepdims=True)
@@ -147,9 +153,9 @@
 ):
     mine = pl.multiple_of(_seat() * TOK, TOK)
 
-    stats = block_ref[:, STATS:, :].reshape(NK * 16, LANES)
-    target = _iota((2 * NK, NK * 16), 0)
-    source = _iota((2 * NK, NK * 16), 1) - (target % NK) * 16 - (target // NK) * 3
+    stats = block_ref[:, STATS:, :].reshape(NK * STAT_ROWS, LANES)
+    target = _iota((2 * NK, NK * STAT_ROWS), 0)
+    source = _iota((2 * NK, NK * STAT_ROWS), 1) - (target % NK) * STAT_ROWS - (target // NK) * 3
     picked = jnp.where((source >= 0) & (source < 3), 1.0, 0.0).astype(BF)
     stats = jnp.dot(picked, stats, preferred_element_type=F32)
     parts_mean, parts_away = stats[:NK], stats[NK:]
@@ -185,8 +191,9 @@
 def attend_kernel(queries_ref, own_queries_ref, hidden_ref, block_ref, key_ref, value_ref, part_ref, own_ref):
     strips = [block_ref[:, part * TOK : (part + 1) * TOK, :].reshape(KROWS, LANES) for part in range(C // LANES)]
     both_hidden = jnp.concatenate([jnp.concatenate(strips, axis=1), hidden_ref[...]], axis=0)
-    both_keys = jnp.dot(both_hidden, key_ref[...], preferred_element_type=F32).astype(BF)
-    both_values = jnp.dot(both_hidden, value_ref[...], preferred_element_type=F32).astype(BF)
+    pair_proj = jnp.concatenate([key_ref[...], value_ref[...]], axis=1)
+    both = jnp.dot(both_hidden, pair_proj, preferred_element_type=F32).astype(BF)
+    both_keys, both_values = both[:, :C], both[:, C:]
     keys, fresh_keys = both_keys[:KROWS], both_keys[KROWS:]
     values, fresh_values = both_values[:KROWS], both_values[KROWS:]
 
@@ -249,7 +256,7 @@
 def on_device(latent, stale_hidden, input_proj, query_proj, key_proj, value_proj, output_proj):
     shape = jax.ShapeDtypeStruct
     latents = _share(latent.reshape(TOK, C), BRICKS)
-    blocks = _call(pack_kernel, shape((NK, STATS + 16, LANES), BF), 2)(latents, stale_hidden)
+    blocks = _call(pack_kernel, shape((NK, STATS + STAT_ROWS, LANES), BF), 2)(latents, stale_hidden)
     blocks = lax.all_to_all(blocks, "patch", 0, 0, axis_index_groups=SEATS)
     queries, own_queries, projected, hidden = _call(
         query_kernel,

time: 64.9 us -> 64 us (0.986)
  no operation moved by 1% of the time
where the time goes in v9:
time: 64 us; the launch traced here: 63.6 us
  blocking collectives  55.5 us (87%)
  Pallas kernels  6.49 us (10%)
  local copies, waits for them, and re-layouts  0.96 us (2%)
  between operations  0.69 us (1%)
    all_to_all x1, blocking collectives, on_device(): blocks = lax.all_to_all(blocks, 'patch', 0, 0, axis_index_groups=SEATS)  30.7 us
    all_to_all x1, blocking collectives, _share(): return lax.all_to_all(copies, 'patch', 0, 0, axis_index_groups=groups)  14 us
    all_to_all x1, blocking collectives, on_device(): parts = lax.all_to_all(parts, 'patch', 0, 0, axis_index_groups=BRICKS)  10.8 us
    pallas_call x1, Pallas kernels, on_device(): _call(attend_kernel, (shape((NQ, TOK, WIDE), BF), shape((TOK, WIDE), BF))...  3.41 us

profile of v9, /device:TPU:8, one launch (start us, length us, event | category | flops | bytes accessed | tf_op | source)
XLA Modules:
  0.0 63.6 jit_solution(6746148133243287512)
XLA Ops:
  0.6 0.8 %broadcast_in_dim.8 = bf16[8,32,640]{2,1,0:T(8,128)(2,1)S(1)} broadcast(bf16[32,640]{1,0:T(8,128)(2,1)} %bitcast.1), dimensions={1,2} | broadcast | bytes 368640 | tf_op jit(solution)/shard_map/broadcast_in_dim | solution.py:252
  1.4 0.0 copy-start.6
  1.5 14.0 %all_to_all.15.latent_ref = bf16[8,32,640]{2,1,0:T(8,128)(2,1)S(1)} all-to-all(bf16[8,32,640]{2,1,0:T(8,128)(2,1)S(1)} %broadcast_in_dim.8), channel_id=1, replica_groups={{0,1,4,5,8,9,12,13},{2,3,6,7,10,11,14,15},{16,17,20,21,24,25,28,29},{18..., dimensions={0} | all-to-all | bytes 655360 | tf_op jit(solution)/shard_map/all_to_all | solution.py:253
  15.4 0.0 copy-done.6
  15.5 0.0 copy-start.4
  15.5 0.7 %shard_map.86 = bf16[16,168,128]{2,1,0:T(8,128)(2,1)S(1)} custom-call(bf16[8,32,640]{2,1,0:T(8,128)(2,1)S(1)} %all_to_all.15.latent_ref, bf16[32,640]{1,0:T(8,128)(2,1)S(1)} %copy-done.6), custom_call_target="tpu_custom_call" | custom-call | tf_op jit(solution)/shard_map/pallas_call | solution.py:259
  16.1 0.0 copy-start.3
  16.1 30.7 %all_to_all.16.block_ref = bf16[16,168,128]{2,1,0:T(8,128)(2,1)S(1)} all-to-all(bf16[16,168,128]{2,1,0:T(8,128)(2,1)S(1)} %shard_map.86), channel_id=1, replica_groups={{0,2,16,18,32,34,48,50,64,66,80,82,96,98,112,114},{1,3,17,19,33,35,49,5..., dimensions={0} | all-to-all | bytes 1376256 | tf_op jit(solution)/shard_map/all_to_all | solution.py:260
  46.8 0.0 copy-done.4
  46.8 0.0 copy-done.3
  46.8 0.0 copy-start
  46.8 0.0 copy-start.1
  46.8 1.2 %shard_map.87 = (bf16[256,640]{1,0:T(8,128)(2,1)S(1)}, bf16[32,640]{1,0:T(8,128)(2,1)S(1)}, f32[32,640]{1,0:T(8,128)S(1)}, bf16[32,640]{1,0:T(8,128)(2,1)S(1)}) custom-call(bf16[8,32,640]{2,1,0:T(8,128)(2,1)S(1)} %all_to_all.15.latent_ref, bf16[16,168,128]{2,1,0:T(8,128)(2,1)S(1)} %all_to_all.16.block_ref, bf16[640,640]{1,0:T(8,128)(2,1)S(1)} %copy-done.3, ...), custom_call_target="tpu_custom_call" | custom-call | tf_op jit(solution)/shard_map/pallas_call | solution.py:261
  48.1 0.0 copy-done
  48.1 0.1 copy-done.1
  48.2 0.0 copy-start.2
  48.2 3.4 %shard_map.88 = (bf16[8,32,768]{2,1,0:T(8,128)(2,1)S(1)}, bf16[32,768]{1,0:T(8,128)(2,1)S(1)}) custom-call(bf16[256,640]{1,0:T(8,128)(2,1)S(1)} %get-tuple-element.8.queries_ref, bf16[32,640]{1,0:T(8,128)(2,1)S(1)} %get-tuple-element.9.own_queries_ref, bf16[32,640]{1,0:T(8,128)(2,1)S(1)} %get-tuple-element.10.hidden_ref, ...), custom_call_target="tpu_custom_call" | custom-call | tf_op jit(solution)/shard_map/pallas_call | solution.py:267
  51.6 0.0 copy-start.5
  51.7 10.8 %all_to_all.17.part_ref = bf16[8,32,768]{2,1,0:T(8,128)(2,1)S(1)} all-to-all(bf16[8,32,768]{2,1,0:T(8,128)(2,1)S(1)} %get-tuple-element.11), channel_id=1, replica_groups={{0,1,4,5,8,9,12,13},{2,3,6,7,10,11,14,15},{16,17,20,21,24,25,28,29},{18..., dimensions={0} | all-to-all | bytes 786432 | tf_op jit(solution)/shard_map/all_to_all | solution.py:270
  62.4 0.0 copy-done.2
  62.4 0.0 copy-done.5
  62.4 1.2 %shard_map.89 = (bf16[1,32,640]{2,1,0:T(8,128)(2,1)}, bf16[32,640]{1,0:T(8,128)(2,1)}) custom-call(bf16[8,32,768]{2,1,0:T(8,128)(2,1)S(1)} %all_to_all.17.part_ref, bf16[32,768]{1,0:T(8,128)(2,1)S(1)} %get-tuple-element.12.own_ref, f32[32,640]{1,0:T(8,128)S(1)} %get-tuple-element.13.projected_ref, bf16[32,640]{1,0:T(8,128)(2,1)S(1)} %get-tuple-element.10.hidden_ref, ...), custom_call_target="tpu_custom_call" | custom-call | tf_op jit(solution)/shard_map/pallas_call | solution.py:271
Async XLA Ops:
  1.4 14.0 %copy-start.6 = (bf16[32,640]{1,0:T(8,128)(2,1)S(1)}, bf16[32,640]{1,0:T(8,128)(2,1)}, u32[]{:S(2)}) copy-start(bf16[32,640]{1,0:T(8,128)(2,1)} %stale_ref.1) | copy-start | bytes 122884
  15.5 31.4 %copy-start.4 = (bf16[640,640]{1,0:T(8,128)(2,1)S(1)}, bf16[640,640]{1,0:T(8,128)(2,1)}, u32[]{:S(2)}) copy-start(bf16[640,640]{1,0:T(8,128)(2,1)} %query_ref.1) | copy-start | bytes 2457604
  16.1 30.7 %copy-start.3 = (bf16[640,640]{1,0:T(8,128)(2,1)S(1)}, bf16[640,640]{1,0:T(8,128)(2,1)}, u32[]{:S(2)}) copy-start(bf16[640,640]{1,0:T(8,128)(2,1)} %input_ref.1) | copy-start | bytes 2457604
  46.8 1.3 %copy-start = (bf16[640,640]{1,0:T(8,128)(2,1)S(1)}, bf16[640,640]{1,0:T(8,128)(2,1)}, u32[]{:S(2)}) copy-start(bf16[640,640]{1,0:T(8,128)(2,1)} %key_ref.1) | copy-start | bytes 2457604
  46.8 1.4 %copy-start.1 = (bf16[640,640]{1,0:T(8,128)(2,1)S(1)}, bf16[640,640]{1,0:T(8,128)(2,1)}, u32[]{:S(2)}) copy-start(bf16[640,640]{1,0:T(8,128)(2,1)} %value_ref.1) | copy-start | bytes 2457604
  48.2 14.2 %copy-start.2 = (bf16[640,640]{1,0:T(8,128)(2,1)S(1)}, bf16[640,640]{1,0:T(8,128)(2,1)}, u32[]{:S(2)}) copy-start(bf16[640,640]{1,0:T(8,128)(2,1)} %output_ref.1) | copy-start | bytes 2457604
  51.6 10.8 %copy-start.5 = (bf16[1,32,640]{2,1,0:T(8,128)(2,1)S(1)}, bf16[1,32,640]{2,1,0:T(8,128)(2,1)}, u32[]{:S(2)}) copy-start(bf16[1,32,640]{2,1,0:T(8,128)(2,1)} %latent_ref.1) | copy-start | bytes 122884

commit v10 on v9

--- a/solution.py
+++ b/solution.py
@@ -74,10 +74,14 @@
         sums = jnp.dot(_stack_pieces(row), to_group, preferred_element_type=F32)
         return jnp.sum(sums, axis=0, keepdims=True)
 
-    center = group_sums(jnp.sum(cells, axis=0, keepdims=True)) * (1.0 / (QROWS * GROUP))
+    pivot = cells[0:1, :]
+    shifted = cells - pivot
+    total = jnp.sum(shifted, axis=0, keepdims=True)
+    mean = pivot + total * (1.0 / QROWS)
+    spread = jnp.sum(jnp.square(shifted), axis=0, keepdims=True) - jnp.square(total) * (1.0 / QROWS)
+    center = group_sums(mean) * (1.0 / GROUP)
     centers = jnp.dot(_stack_pieces(center), to_channel, preferred_element_type=F32)
-    shifted = cells - jnp.sum(centers, axis=0, keepdims=True)
-    away = group_sums(jnp.sum(jnp.square(shifted), axis=0, keepdims=True))
+    away = group_sums(spread + float(QROWS) * jnp.square(mean - jnp.sum(centers, axis=0, keepdims=True)))
     stats = _stack_pieces(center, away, height=STAT_ROWS)
     for index in range(NK):
         for part in range(C // LANES):
@@ -127,9 +131,10 @@
     ones = jnp.ones_like(v_pair)
     sums = jnp.dot(weights, jnp.concatenate([v_pair, ones], axis=1), preferred_element_type=F32)
     total = sums[:, LANES:]
-    mixed = sums[:, :LANES] / total
-    logs = top * STEP + jnp.log2(total)
-    return jnp.where(left, mixed[:rows], mixed[rows:]), logs[:rows], logs[rows:]
+    chosen = jnp.where(left, sums[:rows, :LANES], sums[rows:, :LANES])
+    mixed = chosen / jnp.where(left, total[:rows], total[rows:])
+    top = top * STEP
+    return mixed, (top[:rows], total[:rows]), (top[rows:], total[rows:])
 
 
 def _pack_logs(logs):
@@ -202,13 +207,16 @@
     bias = jnp.where((row_band == _seat()) & (col_band == _brick()), FAR, 0.0).astype(F32)
 
     lane = _iota((QROWS, LANES), 1) % SLOT
-    logs = jnp.zeros((QROWS, LANES), F32)
+    tops = jnp.zeros((QROWS, LANES), F32)
+    totals = jnp.ones((QROWS, LANES), F32)
     for pair in range(HEADS // 2):
         cut = slice(pair * LANES, (pair + 1) * LANES)
         mixed, low, high = _attend(queries_ref[:, cut], keys[:, cut], values[:, cut], bias)
         part_ref[:, :, cut] = mixed.astype(BF).reshape(NQ, TOK, LANES)
-        logs = jnp.where(lane == 2 * pair, low, jnp.where(lane == 2 * pair + 1, high, logs))
-    part_ref[:, :, C:] = _pack_logs(logs).reshape(NQ, TOK, LANES)
+        first, second = lane == 2 * pair, lane == 2 * pair + 1
+        tops = jnp.where(first, low[0], jnp.where(second, high[0], tops))
+        totals = jnp.where(first, low[1], jnp.where(second, high[1], totals))
+    part_ref[:, :, C:] = _pack_logs(tops + jnp.log2(totals)).reshape(NQ, TOK, LANES)
     _attend_own(own_queries_ref[...], fresh_keys, fresh_values, own_ref)
 
 

time: 64 us -> 63.9 us (level)
  no operation moved by 1% of the time
where the time goes in v10:
time: 63.9 us; the launch traced here: 63.5 us
  blocking collectives  55.5 us (87%)
  Pallas kernels  6.39 us (10%)
  local copies, waits for them, and re-layouts  0.97 us (2%)
  between operations  0.69 us (1%)
    all_to_all x1, blocking collectives, on_device(): blocks = lax.all_to_all(blocks, 'patch', 0, 0, axis_index_groups=SEATS)  30.7 us
    all_to_all x1, blocking collectives, _share(): return lax.all_to_all(copies, 'patch', 0, 0, axis_index_groups=groups)  14 us
    all_to_all x1, blocking collectives, on_device(): parts = lax.all_to_all(parts, 'patch', 0, 0, axis_index_groups=BRICKS)  10.8 us
    pallas_call x1, Pallas kernels, on_device(): _call(attend_kernel, (shape((NQ, TOK, WIDE), BF), shape((TOK, WIDE), BF))...  3.36 us

profile of v10, /device:TPU:8, one launch (start us, length us, event | category | flops | bytes accessed | tf_op | source)
XLA Modules:
  0.0 63.5 jit_solution(14659131090363396715)
XLA Ops:
  0.6 0.8 %broadcast_in_dim.8 = bf16[8,32,640]{2,1,0:T(8,128)(2,1)S(1)} broadcast(bf16[32,640]{1,0:T(8,128)(2,1)} %bitcast.1), dimensions={1,2} | broadcast | bytes 368640 | tf_op jit(solution)/shard_map/broadcast_in_dim | solution.py:260
  1.4 0.0 copy-start.6
  1.5 14.0 %all_to_all.15.latent_ref = bf16[8,32,640]{2,1,0:T(8,128)(2,1)S(1)} all-to-all(bf16[8,32,640]{2,1,0:T(8,128)(2,1)S(1)} %broadcast_in_dim.8), channel_id=1, replica_groups={{0,1,4,5,8,9,12,13},{2,3,6,7,10,11,14,15},{16,17,20,21,24,25,28,29},{18..., dimensions={0} | all-to-all | bytes 655360 | tf_op jit(solution)/shard_map/all_to_all | solution.py:261
  15.4 0.0 copy-done.6
  15.5 0.0 copy-start.4
  15.5 0.6 shard_map.86
  16.1 0.0 copy-start.3
  16.1 30.7 %all_to_all.16.block_ref = bf16[16,168,128]{2,1,0:T(8,128)(2,1)S(1)} all-to-all(bf16[16,168,128]{2,1,0:T(8,128)(2,1)S(1)} %shard_map.86), channel_id=1, replica_groups={{0,2,16,18,32,34,48,50,64,66,80,82,96,98,112,114},{1,3,17,19,33,35,49,5..., dimensions={0} | all-to-all | bytes 1376256 | tf_op jit(solution)/shard_map/all_to_all | solution.py:268
  46.8 0.0 copy-done.4
  46.8 0.0 copy-done.3
  46.8 0.0 copy-start
  46.8 0.0 copy-start.1
  46.8 1.2 %shard_map.87 = (bf16[256,640]{1,0:T(8,128)(2,1)S(1)}, bf16[32,640]{1,0:T(8,128)(2,1)S(1)}, f32[32,640]{1,0:T(8,128)S(1)}, bf16[32,640]{1,0:T(8,128)(2,1)S(1)}) custom-call(bf16[8,32,640]{2,1,0:T(8,128)(2,1)S(1)} %all_to_all.15.latent_ref, bf16[16,168,128]{2,1,0:T(8,128)(2,1)S(1)} %all_to_all.16.block_ref, bf16[640,640]{1,0:T(8,128)(2,1)S(1)} %copy-done.3, ...), custom_call_target="tpu_custom_call" | custom-call | tf_op jit(solution)/shard_map/pallas_call | solution.py:269
  48.0 0.0 copy-done
  48.1 0.1 copy-done.1
  48.2 0.0 copy-start.2
  48.2 3.4 %shard_map.88 = (bf16[8,32,768]{2,1,0:T(8,128)(2,1)S(1)}, bf16[32,768]{1,0:T(8,128)(2,1)S(1)}) custom-call(bf16[256,640]{1,0:T(8,128)(2,1)S(1)} %get-tuple-element.8.queries_ref, bf16[32,640]{1,0:T(8,128)(2,1)S(1)} %get-tuple-element.9.own_queries_ref, bf16[32,640]{1,0:T(8,128)(2,1)S(1)} %get-tuple-element.10.hidden_ref, ...), custom_call_target="tpu_custom_call" | custom-call | tf_op jit(solution)/shard_map/pallas_call | solution.py:275
  51.5 0.0 copy-start.5
  51.6 10.8 %all_to_all.17.part_ref = bf16[8,32,768]{2,1,0:T(8,128)(2,1)S(1)} all-to-all(bf16[8,32,768]{2,1,0:T(8,128)(2,1)S(1)} %get-tuple-element.11), channel_id=1, replica_groups={{0,1,4,5,8,9,12,13},{2,3,6,7,10,11,14,15},{16,17,20,21,24,25,28,29},{18..., dimensions={0} | all-to-all | bytes 786432 | tf_op jit(solution)/shard_map/all_to_all | solution.py:278
  62.3 0.0 copy-done.2
  62.3 0.0 copy-done.5
  62.3 1.2 %shard_map.89 = (bf16[1,32,640]{2,1,0:T(8,128)(2,1)}, bf16[32,640]{1,0:T(8,128)(2,1)}) custom-call(bf16[8,32,768]{2,1,0:T(8,128)(2,1)S(1)} %all_to_all.17.part_ref, bf16[32,768]{1,0:T(8,128)(2,1)S(1)} %get-tuple-element.12.own_ref, f32[32,640]{1,0:T(8,128)S(1)} %get-tuple-element.13.projected_ref, bf16[32,640]{1,0:T(8,128)(2,1)S(1)} %get-tuple-element.10.hidden_ref, ...), custom_call_target="tpu_custom_call" | custom-call | tf_op jit(solution)/shard_map/pallas_call | solution.py:279
Async XLA Ops:
  1.4 14.0 %copy-start.6 = (bf16[32,640]{1,0:T(8,128)(2,1)S(1)}, bf16[32,640]{1,0:T(8,128)(2,1)}, u32[]{:S(2)}) copy-start(bf16[32,640]{1,0:T(8,128)(2,1)} %stale_ref.1) | copy-start | bytes 122884
  15.5 31.3 %copy-start.4 = (bf16[640,640]{1,0:T(8,128)(2,1)S(1)}, bf16[640,640]{1,0:T(8,128)(2,1)}, u32[]{:S(2)}) copy-start(bf16[640,640]{1,0:T(8,128)(2,1)} %query_ref.1) | copy-start | bytes 2457604
  16.1 30.7 %copy-start.3 = (bf16[640,640]{1,0:T(8,128)(2,1)S(1)}, bf16[640,640]{1,0:T(8,128)(2,1)}, u32[]{:S(2)}) copy-start(bf16[640,640]{1,0:T(8,128)(2,1)} %input_ref.1) | copy-start | bytes 2457604
  46.8 1.3 %copy-start = (bf16[640,640]{1,0:T(8,128)(2,1)S(1)}, bf16[640,640]{1,0:T(8,128)(2,1)}, u32[]{:S(2)}) copy-start(bf16[640,640]{1,0:T(8,128)(2,1)} %key_ref.1) | copy-start | bytes 2457604
  46.8 1.4 %copy-start.1 = (bf16[640,640]{1,0:T(8,128)(2,1)S(1)}, bf16[640,640]{1,0:T(8,128)(2,1)}, u32[]{:S(2)}) copy-start(bf16[640,640]{1,0:T(8,128)(2,1)} %value_ref.1) | copy-start | bytes 2457604
  48.2 14.2 %copy-start.2 = (bf16[640,640]{1,0:T(8,128)(2,1)S(1)}, bf16[640,640]{1,0:T(8,128)(2,1)}, u32[]{:S(2)}) copy-start(bf16[640,640]{1,0:T(8,128)(2,1)} %output_ref.1) | copy-start | bytes 2457604
  51.5 10.8 %copy-start.5 = (bf16[1,32,640]{2,1,0:T(8,128)(2,1)S(1)}, bf16[1,32,640]{2,1,0:T(8,128)(2,1)}, u32[]{:S(2)}) copy-start(bf16[1,32,640]{2,1,0:T(8,128)(2,1)} %latent_ref.1) | copy-start | bytes 122884

commit v11 on v10

--- a/solution.py
+++ b/solution.py
@@ -74,14 +74,10 @@
         sums = jnp.dot(_stack_pieces(row), to_group, preferred_element_type=F32)
         return jnp.sum(sums, axis=0, keepdims=True)
 
-    pivot = cells[0:1, :]
-    shifted = cells - pivot
-    total = jnp.sum(shifted, axis=0, keepdims=True)
-    mean = pivot + total * (1.0 / QROWS)
-    spread = jnp.sum(jnp.square(shifted), axis=0, keepdims=True) - jnp.square(total) * (1.0 / QROWS)
-    center = group_sums(mean) * (1.0 / GROUP)
+    center = group_sums(jnp.sum(cells, axis=0, keepdims=True)) * (1.0 / (QROWS * GROUP))
     centers = jnp.dot(_stack_pieces(center), to_channel, preferred_element_type=F32)
-    away = group_sums(spread + float(QROWS) * jnp.square(mean - jnp.sum(centers, axis=0, keepdims=True)))
+    shifted = cells - jnp.sum(centers, axis=0, keepdims=True)
+    away = group_sums(jnp.sum(jnp.square(shifted), axis=0, keepdims=True))
     stats = _stack_pieces(center, away, height=STAT_ROWS)
     for index in range(NK):
         for part in range(C // LANES):

time: 63.9 us -> 64 us (level)
  no operation moved by 1% of the time
where the time goes in v11:
time: 64 us; the launch traced here: 63.6 us
  blocking collectives  55.5 us (87%)
  Pallas kernels  6.43 us (10%)
  local copies, waits for them, and re-layouts  0.96 us (2%)
  between operations  0.69 us (1%)
    all_to_all x1, blocking collectives, on_device(): blocks = lax.all_to_all(blocks, 'patch', 0, 0, axis_index_groups=SEATS)  30.7 us
    all_to_all x1, blocking collectives, _share(): return lax.all_to_all(copies, 'patch', 0, 0, axis_index_groups=groups)  14 us
    all_to_all x1, blocking collectives, on_device(): parts = lax.all_to_all(parts, 'patch', 0, 0, axis_index_groups=BRICKS)  10.8 us
    pallas_call x1, Pallas kernels, on_device(): _call(attend_kernel, (shape((NQ, TOK, WIDE), BF), shape((TOK, WIDE), BF))...  3.36 us

profile of v11, /device:TPU:8, one launch (start us, length us, event | category | flops | bytes accessed | tf_op | source)
XLA Modules:
  0.0 63.6 jit_solution(12908441120114831266)
XLA Ops:
  0.6 0.8 %broadcast_in_dim.8 = bf16[8,32,640]{2,1,0:T(8,128)(2,1)S(1)} broadcast(bf16[32,640]{1,0:T(8,128)(2,1)} %bitcast.1), dimensions={1,2} | broadcast | bytes 368640 | tf_op jit(solution)/shard_map/broadcast_in_dim | solution.py:256
  1.4 0.0 copy-start.6
  1.5 14.0 %all_to_all.15.latent_ref = bf16[8,32,640]{2,1,0:T(8,128)(2,1)S(1)} all-to-all(bf16[8,32,640]{2,1,0:T(8,128)(2,1)S(1)} %broadcast_in_dim.8), channel_id=1, replica_groups={{0,1,4,5,8,9,12,13},{2,3,6,7,10,11,14,15},{16,17,20,21,24,25,28,29},{18..., dimensions={0} | all-to-all | bytes 655360 | tf_op jit(solution)/shard_map/all_to_all | solution.py:257
  15.4 0.0 copy-done.6
  15.5 0.0 copy-start.4
  15.5 0.7 %shard_map.86 = bf16[16,168,128]{2,1,0:T(8,128)(2,1)S(1)} custom-call(bf16[8,32,640]{2,1,0:T(8,128)(2,1)S(1)} %all_to_all.15.latent_ref, bf16[32,640]{1,0:T(8,128)(2,1)S(1)} %copy-done.6), custom_call_target="tpu_custom_call" | custom-call | tf_op jit(solution)/shard_map/pallas_call | solution.py:263
  16.1 0.0 copy-start.3
  16.1 30.7 %all_to_all.16.block_ref = bf16[16,168,128]{2,1,0:T(8,128)(2,1)S(1)} all-to-all(bf16[16,168,128]{2,1,0:T(8,128)(2,1)S(1)} %shard_map.86), channel_id=1, replica_groups={{0,2,16,18,32,34,48,50,64,66,80,82,96,98,112,114},{1,3,17,19,33,35,49,5..., dimensions={0} | all-to-all | bytes 1376256 | tf_op jit(solution)/shard_map/all_to_all | solution.py:264
  46.8 0.0 copy-done.4
  46.8 0.0 copy-done.3
  46.8 0.0 copy-start
  46.8 0.0 copy-start.1
  46.8 1.2 %shard_map.87 = (bf16[256,640]{1,0:T(8,128)(2,1)S(1)}, bf16[32,640]{1,0:T(8,128)(2,1)S(1)}, f32[32,640]{1,0:T(8,128)S(1)}, bf16[32,640]{1,0:T(8,128)(2,1)S(1)}) custom-call(bf16[8,32,640]{2,1,0:T(8,128)(2,1)S(1)} %all_to_all.15.latent_ref, bf16[16,168,128]{2,1,0:T(8,128)(2,1)S(1)} %all_to_all.16.block_ref, bf16[640,640]{1,0:T(8,128)(2,1)S(1)} %copy-done.3, ...), custom_call_target="tpu_custom_call" | custom-call | tf_op jit(solution)/shard_map/pallas_call | solution.py:265
  48.1 0.0 copy-done
  48.1 0.1 copy-done.1
  48.2 0.0 copy-start.2
  48.2 3.4 %shard_map.88 = (bf16[8,32,768]{2,1,0:T(8,128)(2,1)S(1)}, bf16[32,768]{1,0:T(8,128)(2,1)S(1)}) custom-call(bf16[256,640]{1,0:T(8,128)(2,1)S(1)} %get-tuple-element.8.queries_ref, bf16[32,640]{1,0:T(8,128)(2,1)S(1)} %get-tuple-element.9.own_queries_ref, bf16[32,640]{1,0:T(8,128)(2,1)S(1)} %get-tuple-element.10.hidden_ref, ...), custom_call_target="tpu_custom_call" | custom-call | tf_op jit(solution)/shard_map/pallas_call | solution.py:271
  51.6 0.0 copy-start.5
  51.6 10.8 %all_to_all.17.part_ref = bf16[8,32,768]{2,1,0:T(8,128)(2,1)S(1)} all-to-all(bf16[8,32,768]{2,1,0:T(8,128)(2,1)S(1)} %get-tuple-element.11), channel_id=1, replica_groups={{0,1,4,5,8,9,12,13},{2,3,6,7,10,11,14,15},{16,17,20,21,24,25,28,29},{18..., dimensions={0} | all-to-all | bytes 786432 | tf_op jit(solution)/shard_map/all_to_all | solution.py:274
  62.4 0.0 copy-done.2
  62.4 0.0 copy-done.5
  62.4 1.2 %shard_map.89 = (bf16[1,32,640]{2,1,0:T(8,128)(2,1)}, bf16[32,640]{1,0:T(8,128)(2,1)}) custom-call(bf16[8,32,768]{2,1,0:T(8,128)(2,1)S(1)} %all_to_all.17.part_ref, bf16[32,768]{1,0:T(8,128)(2,1)S(1)} %get-tuple-element.12.own_ref, f32[32,640]{1,0:T(8,128)S(1)} %get-tuple-element.13.projected_ref, bf16[32,640]{1,0:T(8,128)(2,1)S(1)} %get-tuple-element.10.hidden_ref, ...), custom_call_target="tpu_custom_call" | custom-call | tf_op jit(solution)/shard_map/pallas_call | solution.py:275
Async XLA Ops:
  1.4 14.0 %copy-start.6 = (bf16[32,640]{1,0:T(8,128)(2,1)S(1)}, bf16[32,640]{1,0:T(8,128)(2,1)}, u32[]{:S(2)}) copy-start(bf16[32,640]{1,0:T(8,128)(2,1)} %stale_ref.1) | copy-start | bytes 122884
  15.5 31.4 %copy-start.4 = (bf16[640,640]{1,0:T(8,128)(2,1)S(1)}, bf16[640,640]{1,0:T(8,128)(2,1)}, u32[]{:S(2)}) copy-start(bf16[640,640]{1,0:T(8,128)(2,1)} %query_ref.1) | copy-start | bytes 2457604
  16.1 30.7 %copy-start.3 = (bf16[640,640]{1,0:T(8,128)(2,1)S(1)}, bf16[640,640]{1,0:T(8,128)(2,1)}, u32[]{:S(2)}) copy-start(bf16[640,640]{1,0:T(8,128)(2,1)} %input_ref.1) | copy-start | bytes 2457604
  46.8 1.3 %copy-start = (bf16[640,640]{1,0:T(8,128)(2,1)S(1)}, bf16[640,640]{1,0:T(8,128)(2,1)}, u32[]{:S(2)}) copy-start(bf16[640,640]{1,0:T(8,128)(2,1)} %key_ref.1) | copy-start | bytes 2457604
  46.8 1.4 %copy-start.1 = (bf16[640,640]{1,0:T(8,128)(2,1)S(1)}, bf16[640,640]{1,0:T(8,128)(2,1)}, u32[]{:S(2)}) copy-start(bf16[640,640]{1,0:T(8,128)(2,1)} %value_ref.1) | copy-start | bytes 2457604
  48.2 14.2 %copy-start.2 = (bf16[640,640]{1,0:T(8,128)(2,1)S(1)}, bf16[640,640]{1,0:T(8,128)(2,1)}, u32[]{:S(2)}) copy-start(bf16[640,640]{1,0:T(8,128)(2,1)} %output_ref.1) | copy-start | bytes 2457604
  51.6 10.8 %copy-start.5 = (bf16[1,32,640]{2,1,0:T(8,128)(2,1)S(1)}, bf16[1,32,640]{2,1,0:T(8,128)(2,1)}, u32[]{:S(2)}) copy-start(bf16[1,32,640]{2,1,0:T(8,128)(2,1)} %latent_ref.1) | copy-start | bytes 122884

commit v12 on v11

--- a/solution.py
+++ b/solution.py
@@ -74,10 +74,11 @@
         sums = jnp.dot(_stack_pieces(row), to_group, preferred_element_type=F32)
         return jnp.sum(sums, axis=0, keepdims=True)
 
-    center = group_sums(jnp.sum(cells, axis=0, keepdims=True)) * (1.0 / (QROWS * GROUP))
+    mean = jnp.sum(cells, axis=0, keepdims=True) * (1.0 / QROWS)
+    spread = jnp.sum(jnp.square(cells - mean), axis=0, keepdims=True)
+    center = group_sums(mean) * (1.0 / GROUP)
     centers = jnp.dot(_stack_pieces(center), to_channel, preferred_element_type=F32)
-    shifted = cells - jnp.sum(centers, axis=0, keepdims=True)
-    away = group_sums(jnp.sum(jnp.square(shifted), axis=0, keepdims=True))
+    away = group_sums(spread + float(QROWS) * jnp.square(mean - jnp.sum(centers, axis=0, keepdims=True)))
     stats = _stack_pieces(center, away, height=STAT_ROWS)
     for index in range(NK):
         for part in range(C // LANES):

time: 64 us -> 63.9 us (level)
  no operation moved by 1% of the time
where the time goes in v12:
time: 63.9 us; the launch traced here: 63.5 us
  blocking collectives  55.5 us (87%)
  Pallas kernels  6.35 us (10%)
  local copies, waits for them, and re-layouts  0.97 us (2%)
  between operations  0.69 us (1%)
    all_to_all x1, blocking collectives, on_device(): blocks = lax.all_to_all(blocks, 'patch', 0, 0, axis_index_groups=SEATS)  30.7 us
    all_to_all x1, blocking collectives, _share(): return lax.all_to_all(copies, 'patch', 0, 0, axis_index_groups=groups)  14 us
    all_to_all x1, blocking collectives, on_device(): parts = lax.all_to_all(parts, 'patch', 0, 0, axis_index_groups=BRICKS)  10.8 us
    pallas_call x1, Pallas kernels, on_device(): _call(attend_kernel, (shape((NQ, TOK, WIDE), BF), shape((TOK, WIDE), BF))...  3.36 us

profile of v12, /device:TPU:8, one launch (start us, length us, event | category | flops | bytes accessed | tf_op | source)
XLA Modules:
  0.0 63.5 jit_solution(10349140472733083486)
XLA Ops:
  0.6 0.8 %broadcast_in_dim.8 = bf16[8,32,640]{2,1,0:T(8,128)(2,1)S(1)} broadcast(bf16[32,640]{1,0:T(8,128)(2,1)} %bitcast.1), dimensions={1,2} | broadcast | bytes 368640 | tf_op jit(solution)/shard_map/broadcast_in_dim | solution.py:257
  1.4 0.0 copy-start.6
  1.5 14.0 %all_to_all.15.latent_ref = bf16[8,32,640]{2,1,0:T(8,128)(2,1)S(1)} all-to-all(bf16[8,32,640]{2,1,0:T(8,128)(2,1)S(1)} %broadcast_in_dim.8), channel_id=1, replica_groups={{0,1,4,5,8,9,12,13},{2,3,6,7,10,11,14,15},{16,17,20,21,24,25,28,29},{18..., dimensions={0} | all-to-all | bytes 655360 | tf_op jit(solution)/shard_map/all_to_all | solution.py:258
  15.4 0.0 copy-done.6
  15.5 0.0 copy-start.4
  15.5 0.6 shard_map.86
  16.0 0.0 copy-start.3
  16.0 30.7 %all_to_all.16.block_ref = bf16[16,168,128]{2,1,0:T(8,128)(2,1)S(1)} all-to-all(bf16[16,168,128]{2,1,0:T(8,128)(2,1)S(1)} %shard_map.86), channel_id=1, replica_groups={{0,2,16,18,32,34,48,50,64,66,80,82,96,98,112,114},{1,3,17,19,33,35,49,5..., dimensions={0} | all-to-all | bytes 1376256 | tf_op jit(solution)/shard_map/all_to_all | solution.py:265
  46.7 0.0 copy-done.4
  46.7 0.0 copy-done.3
  46.7 0.0 copy-start
  46.7 0.0 copy-start.1
  46.8 1.2 %shard_map.87 = (bf16[256,640]{1,0:T(8,128)(2,1)S(1)}, bf16[32,640]{1,0:T(8,128)(2,1)S(1)}, f32[32,640]{1,0:T(8,128)S(1)}, bf16[32,640]{1,0:T(8,128)(2,1)S(1)}) custom-call(bf16[8,32,640]{2,1,0:T(8,128)(2,1)S(1)} %all_to_all.15.latent_ref, bf16[16,168,128]{2,1,0:T(8,128)(2,1)S(1)} %all_to_all.16.block_ref, bf16[640,640]{1,0:T(8,128)(2,1)S(1)} %copy-done.3, ...), custom_call_target="tpu_custom_call" | custom-call | tf_op jit(solution)/shard_map/pallas_call | solution.py:266
  48.0 0.0 copy-done
  48.0 0.1 copy-done.1
  48.1 0.0 copy-start.2
  48.1 3.4 %shard_map.88 = (bf16[8,32,768]{2,1,0:T(8,128)(2,1)S(1)}, bf16[32,768]{1,0:T(8,128)(2,1)S(1)}) custom-call(bf16[256,640]{1,0:T(8,128)(2,1)S(1)} %get-tuple-element.8.queries_ref, bf16[32,640]{1,0:T(8,128)(2,1)S(1)} %get-tuple-element.9.own_queries_ref, bf16[32,640]{1,0:T(8,128)(2,1)S(1)} %get-tuple-element.10.hidden_ref, ...), custom_call_target="tpu_custom_call" | custom-call | tf_op jit(solution)/shard_map/pallas_call | solution.py:272
  51.5 0.0 copy-start.5
  51.5 10.8 %all_to_all.17.part_ref = bf16[8,32,768]{2,1,0:T(8,128)(2,1)S(1)} all-to-all(bf16[8,32,768]{2,1,0:T(8,128)(2,1)S(1)} %get-tuple-element.11), channel_id=1, replica_groups={{0,1,4,5,8,9,12,13},{2,3,6,7,10,11,14,15},{16,17,20,21,24,25,28,29},{18..., dimensions={0} | all-to-all | bytes 786432 | tf_op jit(solution)/shard_map/all_to_all | solution.py:275
  62.3 0.0 copy-done.2
  62.3 0.0 copy-done.5
  62.3 1.2 %shard_map.89 = (bf16[1,32,640]{2,1,0:T(8,128)(2,1)}, bf16[32,640]{1,0:T(8,128)(2,1)}) custom-call(bf16[8,32,768]{2,1,0:T(8,128)(2,1)S(1)} %all_to_all.17.part_ref, bf16[32,768]{1,0:T(8,128)(2,1)S(1)} %get-tuple-element.12.own_ref, f32[32,640]{1,0:T(8,128)S(1)} %get-tuple-element.13.projected_ref, bf16[32,640]{1,0:T(8,128)(2,1)S(1)} %get-tuple-element.10.hidden_ref, ...), custom_call_target="tpu_custom_call" | custom-call | tf_op jit(solution)/shard_map/pallas_call | solution.py:276
Async XLA Ops:
  1.4 14.0 %copy-start.6 = (bf16[32,640]{1,0:T(8,128)(2,1)S(1)}, bf16[32,640]{1,0:T(8,128)(2,1)}, u32[]{:S(2)}) copy-start(bf16[32,640]{1,0:T(8,128)(2,1)} %stale_ref.1) | copy-start | bytes 122884
  15.5 31.3 %copy-start.4 = (bf16[640,640]{1,0:T(8,128)(2,1)S(1)}, bf16[640,640]{1,0:T(8,128)(2,1)}, u32[]{:S(2)}) copy-start(bf16[640,640]{1,0:T(8,128)(2,1)} %query_ref.1) | copy-start | bytes 2457604
  16.0 30.7 %copy-start.3 = (bf16[640,640]{1,0:T(8,128)(2,1)S(1)}, bf16[640,640]{1,0:T(8,128)(2,1)}, u32[]{:S(2)}) copy-start(bf16[640,640]{1,0:T(8,128)(2,1)} %input_ref.1) | copy-start | bytes 2457604
  46.7 1.3 %copy-start = (bf16[640,640]{1,0:T(8,128)(2,1)S(1)}, bf16[640,640]{1,0:T(8,128)(2,1)}, u32[]{:S(2)}) copy-start(bf16[640,640]{1,0:T(8,128)(2,1)} %key_ref.1) | copy-start | bytes 2457604
  46.7 1.4 %copy-start.1 = (bf16[640,640]{1,0:T(8,128)(2,1)S(1)}, bf16[640,640]{1,0:T(8,128)(2,1)}, u32[]{:S(2)}) copy-start(bf16[640,640]{1,0:T(8,128)(2,1)} %value_ref.1) | copy-start | bytes 2457604
  48.1 14.2 %copy-start.2 = (bf16[640,640]{1,0:T(8,128)(2,1)S(1)}, bf16[640,640]{1,0:T(8,128)(2,1)}, u32[]{:S(2)}) copy-start(bf16[640,640]{1,0:T(8,128)(2,1)} %output_ref.1) | copy-start | bytes 2457604
  51.5 10.8 %copy-start.5 = (bf16[1,32,640]{2,1,0:T(8,128)(2,1)S(1)}, bf16[1,32,640]{2,1,0:T(8,128)(2,1)}, u32[]{:S(2)}) copy-start(bf16[1,32,640]{2,1,0:T(8,128)(2,1)} %latent_ref.1) | copy-start | bytes 122884

commit v13 on v11

--- a/solution.py
+++ b/solution.py
@@ -32,7 +32,7 @@
 
 
 BRICKS = _groups(lambda y, x, z: (y, z // 2))
-SEATS = _groups(lambda y, x, z: (x, z % 2))
+SEATS = [sorted(group, key=lambda index: (index % 4, index)) for group in _groups(lambda y, x, z: (x, z % 2))]
 NQ = len(BRICKS[0])
 NK = len(SEATS[0])
 QROWS = NQ * TOK
@@ -146,7 +146,7 @@
 
 def _brick():
     me = lax.axis_index("patch")
-    return (me >> 4) * 2 + ((me >> 1) & 1)
+    return ((me >> 1) & 1) * 8 + (me >> 4)
 
 
 def query_kernel(

time: 64 us -> 63.7 us (level)
  no operation moved by 1% of the time
where the time goes in v13:
time: 63.7 us; the launch traced here: 63.3 us
  blocking collectives  55.2 us (87%)
  Pallas kernels  6.43 us (10%)
  local copies, waits for them, and re-layouts  0.97 us (2%)
  between operations  0.69 us (1%)
    all_to_all x1, blocking collectives, on_device(): blocks = lax.all_to_all(blocks, 'patch', 0, 0, axis_index_groups=SEATS)  30.5 us
    all_to_all x1, blocking collectives, _share(): return lax.all_to_all(copies, 'patch', 0, 0, axis_index_groups=groups)  14 us
    all_to_all x1, blocking collectives, on_device(): parts = lax.all_to_all(parts, 'patch', 0, 0, axis_index_groups=BRICKS)  10.6 us
    pallas_call x1, Pallas kernels, on_device(): _call(attend_kernel, (shape((NQ, TOK, WIDE), BF), shape((TOK, WIDE), BF))...  3.36 us

profile of v13, /device:TPU:8, one launch (start us, length us, event | category | flops | bytes accessed | tf_op | source)
XLA Modules:
  0.0 63.3 jit_solution(1320804929675219114)
XLA Ops:
  0.6 0.8 %broadcast_in_dim.8 = bf16[8,32,640]{2,1,0:T(8,128)(2,1)S(1)} broadcast(bf16[32,640]{1,0:T(8,128)(2,1)} %bitcast.1), dimensions={1,2} | broadcast | bytes 368640 | tf_op jit(solution)/shard_map/broadcast_in_dim | solution.py:256
  1.4 0.0 copy-start.6
  1.5 14.0 %all_to_all.15.latent_ref = bf16[8,32,640]{2,1,0:T(8,128)(2,1)S(1)} all-to-all(bf16[8,32,640]{2,1,0:T(8,128)(2,1)S(1)} %broadcast_in_dim.8), channel_id=1, replica_groups={{0,1,4,5,8,9,12,13},{2,3,6,7,10,11,14,15},{16,17,20,21,24,25,28,29},{18..., dimensions={0} | all-to-all | bytes 655360 | tf_op jit(solution)/shard_map/all_to_all | solution.py:257
  15.4 0.0 copy-done.6
  15.5 0.0 copy-start.4
  15.5 0.7 %shard_map.86 = bf16[16,168,128]{2,1,0:T(8,128)(2,1)S(1)} custom-call(bf16[8,32,640]{2,1,0:T(8,128)(2,1)S(1)} %all_to_all.15.latent_ref, bf16[32,640]{1,0:T(8,128)(2,1)S(1)} %copy-done.6), custom_call_target="tpu_custom_call" | custom-call | tf_op jit(solution)/shard_map/pallas_call | solution.py:263
  16.1 0.0 copy-start.3
  16.1 30.5 %all_to_all.16.block_ref = bf16[16,168,128]{2,1,0:T(8,128)(2,1)S(1)} all-to-all(bf16[16,168,128]{2,1,0:T(8,128)(2,1)S(1)} %shard_map.86), channel_id=1, replica_groups={{0,16,32,48,64,80,96,112,2,18,34,50,66,82,98,114},{1,17,33,49,65,81,97,..., dimensions={0} | all-to-all | bytes 1376256 | tf_op jit(solution)/shard_map/all_to_all | solution.py:264
  46.7 0.0 copy-done.4
  46.7 0.0 copy-done.3
  46.7 0.0 copy-start
  46.7 0.0 copy-start.1
  46.7 1.2 %shard_map.87 = (bf16[256,640]{1,0:T(8,128)(2,1)S(1)}, bf16[32,640]{1,0:T(8,128)(2,1)S(1)}, f32[32,640]{1,0:T(8,128)S(1)}, bf16[32,640]{1,0:T(8,128)(2,1)S(1)}) custom-call(bf16[8,32,640]{2,1,0:T(8,128)(2,1)S(1)} %all_to_all.15.latent_ref, bf16[16,168,128]{2,1,0:T(8,128)(2,1)S(1)} %all_to_all.16.block_ref, bf16[640,640]{1,0:T(8,128)(2,1)S(1)} %copy-done.3, ...), custom_call_target="tpu_custom_call" | custom-call | tf_op jit(solution)/shard_map/pallas_call | solution.py:265
  47.9 0.0 copy-done
  47.9 0.1 copy-done.1
  48.1 0.0 copy-start.2
  48.1 3.4 %shard_map.88 = (bf16[8,32,768]{2,1,0:T(8,128)(2,1)S(1)}, bf16[32,768]{1,0:T(8,128)(2,1)S(1)}) custom-call(bf16[256,640]{1,0:T(8,128)(2,1)S(1)} %get-tuple-element.8.queries_ref, bf16[32,640]{1,0:T(8,128)(2,1)S(1)} %get-tuple-element.9.own_queries_ref, bf16[32,640]{1,0:T(8,128)(2,1)S(1)} %get-tuple-element.10.hidden_ref, ...), custom_call_target="tpu_custom_call" | custom-call | tf_op jit(solution)/shard_map/pallas_call | solution.py:271
  51.4 0.0 copy-start.5
  51.5 10.6 %all_to_all.17.part_ref = bf16[8,32,768]{2,1,0:T(8,128)(2,1)S(1)} all-to-all(bf16[8,32,768]{2,1,0:T(8,128)(2,1)S(1)} %get-tuple-element.11), channel_id=1, replica_groups={{0,1,4,5,8,9,12,13},{2,3,6,7,10,11,14,15},{16,17,20,21,24,25,28,29},{18..., dimensions={0} | all-to-all | bytes 786432 | tf_op jit(solution)/shard_map/all_to_all | solution.py:274
  62.1 0.0 copy-done.2
  62.1 0.0 copy-done.5
  62.1 1.2 %shard_map.89 = (bf16[1,32,640]{2,1,0:T(8,128)(2,1)}, bf16[32,640]{1,0:T(8,128)(2,1)}) custom-call(bf16[8,32,768]{2,1,0:T(8,128)(2,1)S(1)} %all_to_all.17.part_ref, bf16[32,768]{1,0:T(8,128)(2,1)S(1)} %get-tuple-element.12.own_ref, f32[32,640]{1,0:T(8,128)S(1)} %get-tuple-element.13.projected_ref, bf16[32,640]{1,0:T(8,128)(2,1)S(1)} %get-tuple-element.10.hidden_ref, ...), custom_call_target="tpu_custom_call" | custom-call | tf_op jit(solution)/shard_map/pallas_call | solution.py:275
Async XLA Ops:
  1.4 14.0 %copy-start.6 = (bf16[32,640]{1,0:T(8,128)(2,1)S(1)}, bf16[32,640]{1,0:T(8,128)(2,1)}, u32[]{:S(2)}) copy-start(bf16[32,640]{1,0:T(8,128)(2,1)} %stale_ref.1) | copy-start | bytes 122884
  15.5 31.2 %copy-start.4 = (bf16[640,640]{1,0:T(8,128)(2,1)S(1)}, bf16[640,640]{1,0:T(8,128)(2,1)}, u32[]{:S(2)}) copy-start(bf16[640,640]{1,0:T(8,128)(2,1)} %query_ref.1) | copy-start | bytes 2457604
  16.1 30.6 %copy-start.3 = (bf16[640,640]{1,0:T(8,128)(2,1)S(1)}, bf16[640,640]{1,0:T(8,128)(2,1)}, u32[]{:S(2)}) copy-start(bf16[640,640]{1,0:T(8,128)(2,1)} %input_ref.1) | copy-start | bytes 2457604
  46.7 1.3 %copy-start = (bf16[640,640]{1,0:T(8,128)(2,1)S(1)}, bf16[640,640]{1,0:T(8,128)(2,1)}, u32[]{:S(2)}) copy-start(bf16[640,640]{1,0:T(8,128)(2,1)} %key_ref.1) | copy-start | bytes 2457604
  46.7 1.4 %copy-start.1 = (bf16[640,640]{1,0:T(8,128)(2,1)S(1)}, bf16[640,640]{1,0:T(8,128)(2,1)}, u32[]{:S(2)}) copy-start(bf16[640,640]{1,0:T(8,128)(2,1)} %value_ref.1) | copy-start | bytes 2457604
  48.1 14.0 %copy-start.2 = (bf16[640,640]{1,0:T(8,128)(2,1)S(1)}, bf16[640,640]{1,0:T(8,128)(2,1)}, u32[]{:S(2)}) copy-start(bf16[640,640]{1,0:T(8,128)(2,1)} %output_ref.1) | copy-start | bytes 2457604
  51.4 10.7 %copy-start.5 = (bf16[1,32,640]{2,1,0:T(8,128)(2,1)S(1)}, bf16[1,32,640]{2,1,0:T(8,128)(2,1)}, u32[]{:S(2)}) copy-start(bf16[1,32,640]{2,1,0:T(8,128)(2,1)} %latent_ref.1) | copy-start | bytes 122884
